TPU v7x, 256 devices: a whole 4x4x8 slice. The times are simulated.
256 devices in a mesh: row: 8 (over z_hi, y), col: 32 (over z_lo, x, core).
Axes of the slice: x: 4, y: 4, z: 8 (z_hi: 2, z_lo: 4; z = z_hi * 4 + z_lo), core: 2. Of those that a mesh axis runs over, the one named last changes fastest.
Arguments:
- fields: float32 [5, 32, 512, 1024], P(None, None, 'col', 'row'), may hold values from -1.5 to 2, as said below
Outputs:
- advanced: float32 [5, 32, 512, 1024], P(None, None, 'col', 'row')
Inputs may be any that keep to these rules, and one draw needn't show every extreme that they name: `fields`: density lies in 0.5 to 2, pressure in 0.25 to 1 and each velocity component in -1.5 to 1.5, independently from cell to cell.
All inputs are finite; a program needn't handle non-finite values.
Results may differ from a plain program's by a relative error of at most 0.00035.
Values sent between devices are 32-bit elements; how exact they have to be, the bound alone decides.
No kernel may reach another device: no remote copies, remote signals or barrier semaphores. Data moves between devices by JAX's collectives and lax.ppermute only.
A program may use at most 64 MiB of HBM per device.

v0:
```python
import jax
import jax.numpy as jnp
from jax import lax
from jax.sharding import PartitionSpec as P

adiabatic = 1.4
time_ratio = 0.03
shock_factor = (adiabatic + 1.0) / (2.0 * adiabatic)
floor_share = 0.1


def take_slice(values, start, stop, direction):
    return lax.slice_in_dim(values, start, stop, axis=direction)


def periodic(values, direction):
    length = values.shape[direction]
    return jnp.concatenate(
        [
            take_slice(values, length - 3, length, direction),
            values,
            take_slice(values, 0, 3, direction),
        ],
        direction,
    )


def reconstruct(padded, direction):
    length = padded.shape[direction]
    near_left = take_slice(padded, 1, length - 2, direction)
    near_right = take_slice(padded, 2, length - 1, direction)
    interface = 7.0 / 12.0 * (near_left + near_right) - 1.0 / 12.0 * (
        take_slice(padded, 0, length - 3, direction) + take_slice(padded, 3, length, direction)
    )
    interface = jnp.clip(
        interface, jnp.minimum(near_left, near_right), jnp.maximum(near_left, near_right)
    )
    centre = take_slice(padded, 2, length - 2, direction)
    below = take_slice(padded, 1, length - 3, direction)
    above = take_slice(padded, 3, length - 1, direction)
    lowest = jnp.minimum(jnp.minimum(below, centre), above)
    highest = jnp.maximum(jnp.maximum(below, centre), above)
    left_edge = take_slice(interface, 0, length - 4, direction)
    right_edge = take_slice(interface, 1, length - 3, direction)
    spread = right_edge - left_edge
    offset = spread * (centre - 0.5 * (left_edge + right_edge))
    ceiling = spread * spread / 6.0
    new_left = jnp.where(offset > ceiling, 3.0 * centre - 2.0 * right_edge, left_edge)
    new_right = jnp.where(offset < -ceiling, 3.0 * centre - 2.0 * left_edge, right_edge)
    new_left = jnp.clip(new_left, lowest, highest)
    new_right = jnp.clip(new_right, lowest, highest)
    cell_count = length - 4
    return (
        take_slice(new_right, 0, cell_count - 1, direction),
        take_slice(new_left, 1, cell_count, direction),
    )


def conserved(primitives):
    density = primitives[0]
    velocity = primitives[1:4]
    momentum = density * velocity
    energy = primitives[4] / (adiabatic - 1.0) + 0.5 * jnp.sum(momentum * velocity, axis=0)
    return jnp.concatenate([density[None], momentum, energy[None]], 0)


def primitive(totals):
    density = totals[0]
    velocity = totals[1:4] / density
    pressure = (adiabatic - 1.0) * (totals[4] - 0.5 * jnp.sum(totals[1:4] * velocity, axis=0))
    return jnp.concatenate([density[None], velocity, pressure[None]], 0)


def riemann(left_state, right_state, normal):
    dens_left = left_state[0]
    dens_right = right_state[0]
    speed_left = left_state[normal]
    speed_right = right_state[normal]
    press_left = left_state[4]
    press_right = right_state[4]
    sound_left = jnp.sqrt(adiabatic * press_left * dens_left)
    sound_right = jnp.sqrt(adiabatic * press_right * dens_right)
    pressure_floor = floor_share * jnp.minimum(press_left, press_right)
    pressure_star = 0.5 * (press_left + press_right)

    def wave_speeds(guess):
        wave_left = sound_left * jnp.sqrt(1.0 + shock_factor * (guess / press_left - 1.0))
        wave_right = sound_right * jnp.sqrt(1.0 + shock_factor * (guess / press_right - 1.0))
        return (wave_left, wave_right)

    for repeat in range(5):
        wave_left, wave_right = wave_speeds(pressure_star)
        pressure_star = jnp.maximum(
            (
                wave_right * press_left
                + wave_left * press_right
                + wave_left * wave_right * (speed_left - speed_right)
            )
            / (wave_left + wave_right),
            pressure_floor,
        )
    wave_left, wave_right = wave_speeds(pressure_star)
    speed_star = (wave_left * speed_left + wave_right * speed_right + press_left - press_right) / (
        wave_left + wave_right
    )
    return (pressure_star, speed_star)


def sweep(padded, direction, normal):
    left_state, right_state = reconstruct(padded, direction)
    pressure_star, speed_star = riemann(left_state, right_state, normal)
    fluxes = jnp.maximum(speed_star, 0.0) * conserved(left_state) + jnp.minimum(
        speed_star, 0.0
    ) * conserved(right_state)
    fluxes = fluxes.at[normal].add(pressure_star)
    fluxes = fluxes.at[4].add(pressure_star * speed_star)
    length = padded.shape[direction]
    interior = take_slice(padded, 3, length - 3, direction)
    flux_count = length - 5
    totals = conserved(interior) - time_ratio * (
        take_slice(fluxes, 1, flux_count, direction)
        - take_slice(fluxes, 0, flux_count - 1, direction)
    )
    return primitive(totals)


def on_device(fields):
    updated = sweep(
        periodic(lax.all_to_all(fields, "row", split_axis=1, concat_axis=3, tiled=True), 3), 3, 2
    )
    after_y = lax.all_to_all(updated, "row", split_axis=3, concat_axis=1, tiled=True)
    updated = sweep(
        periodic(lax.all_to_all(after_y, "col", split_axis=1, concat_axis=2, tiled=True), 2), 2, 3
    )
    return lax.all_to_all(updated, "col", split_axis=2, concat_axis=1, tiled=True)


def solution(mesh):
    return jax.shard_map(
        on_device,
        mesh=mesh,
        in_specs=(P(None, None, "col", "row"),),
        out_specs=P(None, None, "col", "row"),
        check_vma=False,
    )
```

profile of v0, /device:TPU:24, one launch (start us, length us, event | category | flops | bytes accessed | tf_op | source)
XLA Modules:
  0.0 221.1 jit_solution(13351144145577107250)
XLA Ops:
  0.0 1.4 copy.254
  1.4 34.6 %all_to_all.60 = f32[5,32,16,128]{3,2,0,1:T(8,128)S(1)} all-to-all(f32[5,32,16,128]{3,2,0,1:T(8,128)S(1)} %copy.254), channel_id=1, replica_groups=mesh['row'=8,'col'=32] {'row'}, dimensions={1} | all-to-all | bytes 2621440 | tf_op jit(solution)/shard_map/all_to_all | solution.py:129
  36.0 0.1 copy.255
  36.1 0.8 fusion.101
  37.0 0.9 copy.257
  37.8 0.9 copy.256
  38.7 0.8 copy.263
  39.4 0.2 all_to_all.47
  39.6 0.1 fusion.102
  39.7 1.0 concatenate.84
  40.7 1.2 fusion.4
  41.9 1.8 maximum_minimum_fusion
  43.7 0.8 maximum_minimum_fusion.1
  44.6 2.8 %maximum_bitcast_fusion = (f32[4,16,1025]{2,1,0:T(8,128)S(1)}, f32[1,4,16,1025]{3,2,1,0:T(8,128)S(1)}, f32[1,4,16,1025]{3,2,1,0:T(8,128)S(1)}, f32[4,16,1025]{2,...) fusion(f32[5,4,16,1026]{3,2,1,0:T(8,128)S(1)} %get-tuple-element.72,, ...), kind=kLoop, calls=%fused_computation.77 | loop fusion | flops 8003200 | bytes 3411200 | tf_op jit(solution)/shard_map/mul | solution.py:112
  47.4 0.4 multiply_reduce_fusion
  47.8 0.1 bitcast_add_fusion
  48.0 0.1 bitcast_add_fusion.1
  48.0 0.2 fusion.7
  48.2 0.0 copy-start.1
  48.3 0.1 fusion.23
  48.3 0.1 fusion.22
  48.5 1.1 copy-done.1
  49.6 0.0 copy-done.4
  49.6 0.8 slice_bitcast_fusion
  50.5 1.0 broadcast_multiply_fusion.1
  51.5 0.9 copy.260
  52.3 1.0 mul.1521
  53.3 0.2 copy.259
  53.6 0.1 bitcast_multiply_fusion
  53.7 0.1 copy_add_fusion
  53.7 0.4 fusion.19
  54.2 0.1 multiply_reduce_fusion.5
  54.3 0.1 fusion.100
  54.4 0.1 pad_maximum_fusion.5
  54.5 6.6 %copy.264 = f32[5,4,16,1024]{2,1,0,3:T(4,128)} copy(f32[5,4,16,1024]{3,2,1,0:T(8,128)S(1)} %pad_maximum_fusion.5) | data formatting | bytes 2621440 | tf_op jit(solution)/shard_map/concatenate | solution.py:71
  61.1 10.5 %reshape.1005 = f32[8,1,40960]{2,1,0:T(1,128)S(1)} reshape(f32[1024,5,4,16]{3,2,1,0:T(4,128)} %bitcast.289) | data formatting | bytes 2621440
  71.6 23.3 %all_to_all.61 = f32[8,1,40960]{2,1,0:T(1,128)S(1)} all-to-all(f32[8,1,40960]{2,1,0:T(1,128)S(1)} %reshape.1005), channel_id=1, replica_groups=mesh['row'=8,'col'=32] {'row'}, dimensions={0} | all-to-all | bytes 2621440 | tf_op jit(solution)/shard_map/all_to_all | solution.py:131
  94.9 0.5 broadcast.1022
  95.4 3.8 %reduce.13 = f32[8,40960]{1,0:T(8,128)S(1)} reduce(f32[8,1,40960]{2,1,0:T(1,128)S(1)} %all_to_all.61, f32[]{:T(128)} %broadcast.1022), dimensions={1}, to_apply=%all_to_all.48.reduce_sub_computation | reduce | bytes 2621444 | tf_op jit(solution)/shard_map/all_to_all | solution.py:131
  99.2 11.3 %reshape.1006 = f32[1024,5,4,16]{3,2,1,0:T(4,128)} reshape(f32[8,40960]{1,0:T(8,128)S(1)} %reduce.13) | data formatting | bytes 2621440
  110.5 7.4 %copy.306 = f32[5,4,16,8,128]{4,2,0,1,3:T(8,128)S(1)} copy(f32[5,4,16,8,128]{2,1,0,4,3:T(4,128)} %bitcast.290) | data formatting | bytes 2621440 | tf_op jit(solution)/shard_map/all_to_all | solution.py:131
  117.9 56.3 %all_to_all.62 = f32[5,32,16,128]{3,2,0,1:T(8,128)S(1)} all-to-all(f32[5,32,16,128]{3,2,0,1:T(8,128)S(1)} %bitcast.300), channel_id=1, replica_groups=mesh['row'=8,'col'=32] {'col'}, dimensions={1} | all-to-all | bytes 2621440 | tf_op jit(solution)/shard_map/all_to_all | solution.py:133
  174.3 0.1 fusion.97
  174.3 0.1 fusion.98
  174.5 0.1 copy.268
  174.6 0.1 pad_maximum_fusion.4
  174.7 0.7 fusion.12
  175.4 1.3 maximum_minimum_fusion.2
  176.7 0.1 multiply_reduce_fusion.2
  176.9 0.8 maximum_minimum_fusion.3
  177.7 2.4 %maximum_bitcast_fusion.1 = (f32[513,128]{1,0:T(8,128)S(1)}, f32[1,1,513,128]{3,2,0,1:T(8,128)S(1)}, f32[1,1,513,128]{3,2,1,0:T(8,128)S(1)}, f32[1,1,513,128]{3,2,1,0:T(8,128)S(1)}) fusion(f32[5,1,514,128]{3,2,1,0:T(8,128)S(1)} %get-tuple-element.60, f32[5,1,514,128]{3,2,0,1:T(8,128)S(1)} %bitcast.296, f32[5,1,514,128]{3,2,1,0:T(8,128)S(1)} %maximum_minimum_fusion.3, ...), kind=kLoop, calls=%fused_computation.172 | loop fusion | flops 8208000 | bytes 2889216 | tf_op jit(solution)/shard_map/mul | solution.py:112
  180.1 0.1 multiply_reduce_fusion.3
  180.2 0.2 fusion.15
  180.5 0.1 fusion.26
  180.5 0.1 copy.315
  180.6 0.1 fusion.25
  180.7 0.1 bitcast_multiply_fusion.1
  180.8 0.2 fusion.17
  181.1 0.1 multiply_reduce_fusion.4
  181.2 0.1 fusion.96
  181.2 0.1 pad_maximum_fusion.6
  181.3 1.3 copy.301
  182.7 37.2 %all_to_all.63 = f32[5,1,512,128]{3,1,0,2:T(1,128)S(1)} all-to-all(f32[5,1,512,128]{3,1,0,2:T(1,128)S(1)} %copy.301), channel_id=1, replica_groups=mesh['row'=8,'col'=32] {'col'}, dimensions={2} | all-to-all | bytes 2621440 | tf_op jit(solution)/shard_map/all_to_all | solution.py:135
  219.9 1.1 copy.302
  (19 shorter events, 0.4 us)
Async XLA Ops:
  36.1 2.6 %copy-start = (f32[5,32,16,128]{3,2,1,0:T(8,128)}, f32[5,32,16,128]{3,2,1,0:T(8,128)S(1)}, u32[]{:S(2)}) copy-start(f32[5,32,16,128]{3,2,1,0:T(8,128)S(1)} %copy.255) | copy-start | bytes 3932164
  48.2 1.3 copy-start.1
  48.3 1.3 copy-start.4
  48.5 2.0 copy-start.3
  50.4 3.1 %copy-start.2 = (f32[1,4,16,8,128]{4,3,0,2,1:T(8,128)S(1)}, f32[1,4,16,8,128]{4,3,0,2,1:T(8,128)}, u32[]{:S(2)}) copy-start(f32[1,4,16,8,128]{4,3,0,2,1:T(8,128)} %copy.256) | copy-start | bytes 786436
where the time goes:
time: 225 us; the launch traced here: 221 us
  blocking collectives  151 us (67%)
  local copies, waits for them, and re-layouts  47.6 us (21%)
  other arithmetic  21.6 us (10%)
    all_to_all x1, blocking collectives, on_device(): lax.all_to_all(after_y, 'col', split_axis=1, concat_axis=2, tiled=True)  56.3 us
    all_to_all x1, blocking collectives, on_device(): lax.all_to_all(updated, 'col', split_axis=2, concat_axis=1, tiled=True)  37.2 us
    all_to_all x1, blocking collectives, on_device(): lax.all_to_all(fields, 'row', split_axis=1, concat_axis=3, tiled=True)  34.6 us
    unnamed x14, local copies, waits for them, and re-layouts  24.4 us
    all_to_all x1, blocking collectives, on_device(): lax.all_to_all(updated, 'row', split_axis=3, concat_axis=1, tiled=True)  23.3 us
    all_to_all x2, local copies, waits for them, and re-layouts, on_device(): lax.all_to_all(updated, 'row', split_axis=3, concat_axis=1, tiled=True)  7.94 us
    concatenate x2, local copies, waits for them, and re-layouts, primitive(): return jnp.concatenate([density[None], velocity, pressure[None]], 0)  7.92 us
    mul x2, other arithmetic, sweep(): jnp.maximum(speed_star, 0.0) * conserved(left_state)  5.17 us

commit v1 on v0

v1 whole, which is shorter than its diff:
```python
import jax
import jax.numpy as jnp
from jax import lax
from jax.experimental import pallas as pl
from jax.experimental.pallas import tpu as pltpu
from jax.sharding import PartitionSpec as P

adiabatic = 1.4
time_ratio = 0.03
shock_factor = (adiabatic + 1.0) / (2.0 * adiabatic)
floor_share = 0.1
F32 = jnp.float32
SIDE = 3


def reciprocal(values):
    return pl.reciprocal(values, approx=True)


def edges(cells, count):
    far_left, near_left = cells[: count + 3], cells[1 : count + 4]
    near_right, far_right = cells[2 : count + 5], cells[3:]
    face = (7.0 / 12.0) * (near_left + near_right) - (1.0 / 12.0) * (far_left + far_right)
    face = jnp.maximum(face, jnp.minimum(near_left, near_right))
    face = jnp.minimum(face, jnp.maximum(near_left, near_right))
    centre = cells[2 : count + 4]
    left, right = face[: count + 2], face[1:]
    spread = right - left
    below = centre - left
    above = right - centre
    twice_below = below + below
    twice_above = above + above
    monotone = below * above > 0.0
    new_left = jnp.where(
        spread * (below - twice_above) > 0.0,
        centre - jnp.where(monotone, twice_above, 0.0),
        left,
    )
    new_right = jnp.where(
        spread * (twice_below - above) < 0.0,
        centre + jnp.where(monotone, twice_below, 0.0),
        right,
    )
    return new_right[: count + 1], new_left[1:]


def star(dens_left, speed_left, press_left, dens_right, speed_right, press_right):
    scale = adiabatic * shock_factor
    offset = (1.0 - shock_factor) / shock_factor
    scale_left = scale * dens_left
    scale_right = scale * dens_right
    shift_left = offset * press_left
    shift_right = offset * press_right
    jump = speed_left - speed_right
    floor = floor_share * jnp.minimum(press_left, press_right)
    guess = 0.5 * (press_left + press_right)
    for _ in range(5):
        slow_left = lax.rsqrt(scale_left * (guess + shift_left))
        slow_right = lax.rsqrt(scale_right * (guess + shift_right))
        guess = (press_left * slow_left + press_right * slow_right + jump) * reciprocal(
            slow_left + slow_right
        )
        guess = jnp.maximum(guess, floor)
    slow_left = lax.rsqrt(scale_left * (guess + shift_left))
    slow_right = lax.rsqrt(scale_right * (guess + shift_right))
    speed = (
        slow_right * speed_left
        + slow_left * speed_right
        + (press_left - press_right) * (slow_left * slow_right)
    ) * reciprocal(slow_left + slow_right)
    return guess, speed


def advance(cells, count, normal):
    pairs = [edges(c, count) for c in cells]
    left = [p[0] for p in pairs]
    right = [p[1] for p in pairs]
    press_star, speed_star = star(left[0], left[normal], left[4], right[0], right[normal], right[4])
    upwind = speed_star > 0.0
    state = [jnp.where(upwind, a, b) for a, b in zip(left, right)]
    speed = time_ratio * speed_star
    mass = speed * state[0]
    kinetic = 0.5 * (state[1] * state[1] + state[2] * state[2] + state[3] * state[3])
    fluxes = [mass] + [mass * state[i] for i in (1, 2, 3)]
    fluxes[normal] = fluxes[normal] + time_ratio * press_star
    fluxes.append(
        speed * ((1.0 / (adiabatic - 1.0)) * state[4] + press_star) + mass * kinetic
    )
    mid = [c[3 : count + 3] for c in cells]
    change = [f[1:] - f[:-1] for f in fluxes]
    momentum = [mid[0] * mid[i] for i in (1, 2, 3)]
    energy = (1.0 / (adiabatic - 1.0)) * mid[4] + 0.5 * (
        momentum[0] * mid[1] + momentum[1] * mid[2] + momentum[2] * mid[3]
    )
    density = mid[0] - change[0]
    momentum = [m - c for m, c in zip(momentum, change[1:4])]
    energy = energy - change[4]
    thin = reciprocal(density)
    velocity = [m * thin for m in momentum]
    pressure = (adiabatic - 1.0) * (
        energy
        - 0.5 * (momentum[0] * velocity[0] + momentum[1] * velocity[1] + momentum[2] * velocity[2])
    )
    return [density] + velocity + [pressure]


def to_lines(x_ref, lines_ref):
    for f in range(5):
        for b in range(4):
            turned = x_ref[f, b * 128 : (b + 1) * 128, :].T
            lines_ref[f, b * 64 : (b + 1) * 64, :] = turned[:64]
            lines_ref[f, 256 + b * 64 : 256 + (b + 1) * 64, :] = turned[64:]


def swap_halves(tile):
    return pltpu.roll(tile, 4, 0)


def pack_y(x_ref, first_ref, last_ref, lines_ref):
    to_lines(x_ref, lines_ref)
    for f in range(5):
        for k in range(3):
            first_ref[f, k] = swap_halves(lines_ref[f, pl.ds(k, 8, stride=64), :])
            last_ref[f, k] = swap_halves(lines_ref[f, pl.ds(61 + k, 8, stride=64), :])


Y_CHUNK = 10


def inner_y(x_ref, new_ref, lines_ref, old_ref):
    to_lines(x_ref, lines_ref)
    for f in range(5):
        for k in range(64):
            old_ref[f, k] = lines_ref[f, pl.ds(k, 8, stride=64), :]
    for f in range(5):
        for k in (0, 1, 2, 61, 62, 63):
            new_ref[f, k] = old_ref[f, k]

    def step(i, carry):
        at = jnp.minimum(i * Y_CHUNK, 58 - Y_CHUNK)
        cells = [old_ref[f, pl.ds(at, Y_CHUNK + 6)] for f in range(5)]
        out = advance(cells, Y_CHUNK, 2)
        for f in range(5):
            new_ref[f, pl.ds(at + 3, Y_CHUNK)] = out[f]
        return carry

    lax.fori_loop(0, -(-58 // Y_CHUNK), step, 0)


def outer_y(x_ref, new_ref, before_ref, after_ref, z_ref, first_ref, last_ref, lines_ref, nat_ref):
    to_lines(x_ref, lines_ref)
    low = lax.broadcasted_iota(jnp.int32, (8, 128), 0) < 4
    left, right = [], []
    for f in range(5):
        tile = lambda k: lines_ref[f, pl.ds(k, 8, stride=64), :]
        head = [tile(k) for k in range(6)]
        tail = [tile(58 + k) for k in range(6)]
        before = [jnp.where(low, before_ref[f, k], swap_halves(tail[3 + k])) for k in range(3)]
        after = [jnp.where(low, swap_halves(head[k]), after_ref[f, k]) for k in range(3)]
        left.append(jnp.stack(before + head))
        right.append(jnp.stack(tail + after))
    for cells, base in ((left, 0), (right, 61)):
        out = advance(cells, 3, 2)
        for f in range(5):
            for k in range(3):
                lines_ref[f, pl.ds(base + k, 8, stride=64), :] = out[f][k]
    for f in range(5):
        for k in range(3, 61):
            lines_ref[f, pl.ds(k, 8, stride=64), :] = new_ref[f, k]
        for b in range(4):
            turned = jnp.concatenate(
                [
                    lines_ref[f, b * 64 : (b + 1) * 64, :],
                    lines_ref[f, 256 + b * 64 : 256 + (b + 1) * 64, :],
                ]
            )
            nat_ref[f, b * 128 : (b + 1) * 128, :] = turned.T
    for f in range(5):
        for g in range(4):
            for z in range(16):
                tile = nat_ref[f, pl.ds(128 * g + z, 8, stride=16), :]
                z_ref[f, g, z] = tile
                if z < 3:
                    first_ref[f, g, z] = tile
                if z >= 13:
                    last_ref[f, g, z - 13] = tile


def inner_z(z_ref, new_ref):
    def step(g, carry):
        cells = [z_ref[f, g] for f in range(5)]
        out = advance(cells, 10, 3)
        for f in range(5):
            new_ref[f, g] = out[f]
        return carry

    lax.fori_loop(0, 4, step, 0)


def outer_z(z_ref, new_ref, before_ref, after_ref, out_ref):
    def step(g, carry):
        row = pl.multiple_of(128 * g, 128)
        for f in range(5):
            for z in range(10):
                out_ref[f, pl.ds(row + 3 + z, 8, stride=16), :] = new_ref[f, g, z]
        left = [jnp.concatenate([before_ref[f, g], z_ref[f, g, 0:6]]) for f in range(5)]
        right = [jnp.concatenate([z_ref[f, g, 10:16], after_ref[f, g]]) for f in range(5)]
        for cells, base in ((left, 0), (right, 13)):
            out = advance(cells, 3, 3)
            for f in range(5):
                for z in range(3):
                    out_ref[f, pl.ds(row + base + z, 8, stride=16), :] = out[f][z]
        return carry

    lax.fori_loop(0, 4, step, 0)


def tiles(*shape):
    return jax.ShapeDtypeStruct(shape + (8, 128), F32)


def kernel(body, outs, scratch=(), flops=10**7):
    return pl.pallas_call(
        body,
        out_shape=outs,
        scratch_shapes=[pltpu.VMEM(s, F32) for s in scratch],
        compiler_params=pltpu.CompilerParams(vmem_limit_bytes=24 << 20),
        cost_estimate=pl.CostEstimate(flops=flops, bytes_accessed=1 << 22, transcendentals=flops // 20),
    )


LINES = (5, 512, 128)


def shift(values, axis, by):
    size = lax.axis_size(axis)
    return lax.ppermute(values, axis, [(i, (i + by) % size) for i in range(size)])


def on_device(fields):
    x = fields.reshape(LINES)
    first, last = kernel(pack_y, (tiles(5, 3), tiles(5, 3)), [LINES])(x)
    before = shift(last, "row", 1)
    after = shift(first, "row", -1)
    inner = kernel(inner_y, tiles(5, 64), [LINES, (5, 64, 8, 128)], 10**9)(x)
    state, first, last = kernel(
        outer_y, (tiles(5, 4, 16), tiles(5, 4, 3), tiles(5, 4, 3)), [LINES, LINES]
    )(x, inner, before, after)
    before = shift(last, "col", 1)
    after = shift(first, "col", -1)
    inner = kernel(inner_z, tiles(5, 4, 10), (), 10**9)(state)
    out = kernel(outer_z, jax.ShapeDtypeStruct(LINES, F32))(state, inner, before, after)
    return out.reshape(fields.shape)


def solution(mesh):
    return jax.shard_map(
        on_device,
        mesh=mesh,
        in_specs=(P(None, None, "col", "row"),),
        out_specs=P(None, None, "col", "row"),
        check_vma=False,
    )
```

time: 225 us -> 33.4 us (0.15); the launches traced: 221 us -> 33.3 us
  blocking collectives: 151 us -> 0 us
  local copies, waits for them, and re-layouts: 47.6 us -> 1.32 us
  other arithmetic: 21.6 us -> 0 us
  starting transfers between devices: 0 us -> 12.7 us
  Pallas kernels: 0 us -> 11.1 us
  waiting for transfers between devices: 0 us -> 8.2 us
    all_to_all x4 -> x0, blocking collectives: 151 us -> none  [the longest x1 56.3 us: on_device(): lax.all_to_all(after_y, 'col', split_axis=1, concat_axis=2, tiled=True)]
    unnamed x14 -> x2, local copies, waits for them, and re-layouts: 24.4 us -> 1.32 us
    ppermute x0 -> x4, starting transfers between devices: none -> 12.7 us  [shift(): lax.ppermute(values, axis, [(i, (i + by) % size) for i in range(size)])]
    pallas_call x0 -> x5, Pallas kernels: none -> 11.1 us  [the longest x1 3.97 us: on_device(): inner = kernel(inner_y, tiles(5, 64), [LINES, (5, 64, 8, 128)], 10 ** 9)(x)]
    all_to_all x7 -> x0, local copies, waits for them, and re-layouts: 10.3 us -> none  [the longest x2 7.94 us: on_device(): lax.all_to_all(updated, 'row', split_axis=3, concat_axis=1, tiled=True)]
    concatenate x3 -> x0, local copies, waits for them, and re-layouts: 8.88 us -> none  [the longest x2 7.92 us: primitive(): return jnp.concatenate([density[None], velocity, pressure[None]], 0)]
    ppermute x0 -> x4, waiting for transfers between devices: none -> 8.2 us  [shift(): lax.ppermute(values, axis, [(i, (i + by) % size) for i in range(size)])]
    min x6 -> x0, other arithmetic: 6.6 us -> none  [the longest x2 3.12 us: reconstruct(): new_left = jnp.clip(new_left, lowest, highest)]
  transfers between devices with their start and end apart: 0 -> 4, of which waited for: 0 -> 2; matrix products, arithmetic and copies ran while one was open for 0% -> 0% of each run, Pallas kernels for 0% -> 18%
where the time goes in v1:
time: 33.4 us; the launch traced here: 33.3 us
  starting transfers between devices  12.7 us (38%)
  Pallas kernels  11.1 us (33%)
  waiting for transfers between devices  8.2 us (25%)
  local copies, waits for them, and re-layouts  1.32 us (4%)
    ppermute x4, starting transfers between devices, shift(): lax.ppermute(values, axis, [(i, (i + by) % size) for i in range(size)])  12.7 us
    ppermute x4, waiting for transfers between devices, shift(): lax.ppermute(values, axis, [(i, (i + by) % size) for i in range(size)])  8.2 us
    pallas_call x1, Pallas kernels, on_device(): inner = kernel(inner_y, tiles(5, 64), [LINES, (5, 64, 8, 128)], 10 ** 9)(x)  3.97 us
    pallas_call x1, Pallas kernels, on_device(): kernel(outer_z, jax.ShapeDtypeStruct(LINES, F32))  2.86 us
    pallas_call x1, Pallas kernels, on_device(): inner = kernel(inner_z, tiles(5, 4, 10), (), 10 ** 9)(state)  1.96 us
    pallas_call x1, Pallas kernels, on_device(): kernel(outer_y, (tiles(5, 4, 16), tiles(5, 4, 3), tiles(5, 4, 3)), [LINES...  1.86 us
    unnamed x2, local copies, waits for them, and re-layouts  1.32 us
  transfers between devices with their start and end apart: 4, of which 2 were waited for; matrix products, arithmetic and copies ran while one was open for 0% of the time, Pallas kernels for 18%

profile of v1, /device:TPU:24, one launch (start us, length us, event | category | flops | bytes accessed | tf_op | source)
XLA Modules:
  0.0 33.3 jit_solution(17366523917350685407)
XLA Ops:
  0.0 0.0 copy-start
  0.0 1.3 %copy-done = f32[5,32,16,128]{3,2,1,0:T(8,128)S(1)} copy-done((f32[5,32,16,128]{3,2,1,0:T(8,128)S(1)}, f32[5,32,16,128]{3,2,1,0:T(8,128)}, u32[]{:S(2)}) %copy-start) | copy-done | bytes 1310744
  1.3 0.4 %shard_map.18 = (f32[5,3,8,128]{3,2,1,0:T(8,128)S(1)}, f32[5,3,8,128]{3,2,1,0:T(8,128)S(1)}) custom-call(f32[5,512,128]{2,1,0:T(8,128)S(1)} %bitcast.2), custom_call_target="tpu_custom_call" | custom-call | flops 10000000 | bytes 4194304 | tf_op jit(solution)/shard_map/pallas_call | solution.py:242
  1.8 6.9 %collective-permute-start = (f32[5,3,8,128]{3,2,1,0:T(8,128)S(1)}, f32[5,3,8,128]{3,2,1,0:T(8,128)S(1)}, u32[]{:S(2)}, u32[]{:S(2)}) collective-permute-start(f32[5,3,8,128]{3,2,1,0:T(8,128)S(1)} %get-tuple-element.10), channel_id=1, source_target_pairs={{0,32},{32,64},{64,96},{96,128},{128,160},{160,192},{192,224},{224... | collective-permute-start | bytes 184328 | tf_op jit(solution)/shard_map/ppermute | solution.py:237
  8.7 0.0 collective-permute-start.1
  8.7 4.0 %shard_map.17.new_ref = f32[5,64,8,128]{3,2,1,0:T(8,128)S(1)} custom-call(f32[5,512,128]{2,1,0:T(8,128)S(1)} %bitcast.3), custom_call_target="tpu_custom_call" | custom-call | flops 1000000000 | bytes 4194304 | tf_op jit(solution)/shard_map/pallas_call | solution.py:245
  12.7 0.0 collective-permute-done.before_ref
  12.7 6.3 %collective-permute-done.1.after_ref = f32[5,3,8,128]{3,2,1,0:T(8,128)S(1)} collective-permute-done((f32[5,3,8,128]{3,2,1,0:T(8,128)S(1)}, f32[5,3,8,128]{3,2,1,0:T(8,128)S(1)}, u32[]{:S(2)}, u32[]{:S(2)}) %collective-permute-start.1) | collective-permute-done | bytes 61472 | tf_op jit(solution)/shard_map/ppermute | solution.py:237
  19.0 1.9 %shard_map.19 = (f32[5,4,16,8,128]{4,3,2,1,0:T(8,128)S(1)}, f32[5,4,3,8,128]{4,3,2,1,0:T(8,128)S(1)}, f32[5,4,3,8,128]{4,3,2,1,0:T(8,128)S(1)}) custom-call(f32[5,512,128]{2,1,0:T(8,128)S(1)} %bitcast.4, f32[5,64,8,128]{3,2,1,0:T(8,128)S(1)} %shard_map.17.new_ref, f32[5,3,8,128]{3,2,1,0:T(8,128)S(1)} %collective-permute-done.before_ref, ...), custom_call_target="tpu_custom_call" | custom-call | flops 10000000 | bytes 4194304 | tf_op jit(solution)/shard_map/pallas_call | solution.py:246
  20.8 0.1 collective-permute-start.2
  20.9 5.6 %collective-permute-start.3 = (f32[5,4,3,8,128]{4,3,2,1,0:T(8,128)S(1)}, f32[5,4,3,8,128]{4,3,2,1,0:T(8,128)S(1)}, u32[]{:S(2)}, u32[]{:S(2)}) collective-permute-start(f32[5,4,3,8,128]{4,3,2,1,0:T(8,128)S(1)} %get-tuple-element.14), channel_id=1, source_target_pairs={{0,31},{1,0},{2,1},{3,2},{4,3},{5,4},{6,5},{7,6},{8,7},{9,8},{10,9... | collective-permute-start | bytes 737288 | tf_op jit(solution)/shard_map/ppermute | solution.py:237
  26.6 2.0 %shard_map.20.new_ref = f32[5,4,10,8,128]{4,3,2,1,0:T(8,128)S(1)} custom-call(f32[5,4,16,8,128]{4,3,2,1,0:T(8,128)S(1)} %get-tuple-element.12.z_ref), custom_call_target="tpu_custom_call" | custom-call | flops 1000000000 | bytes 4194304 | tf_op jit(solution)/shard_map/pallas_call | solution.py:251
  28.5 1.9 %collective-permute-done.2.before_ref = f32[5,4,3,8,128]{4,3,2,1,0:T(8,128)S(1)} collective-permute-done((f32[5,4,3,8,128]{4,3,2,1,0:T(8,128)S(1)}, f32[5,4,3,8,128]{4,3,2,1,0:T(8,128)S(1)}, u32[]{:S(2)}, u32[]{:S(2)}) %collective-permute-start.2) | collective-permute-done | bytes 245792 | tf_op jit(solution)/shard_map/ppermute | solution.py:237
  30.4 0.0 collective-permute-done.3.after_ref
  30.4 2.9 %shard_map.21 = f32[5,512,128]{2,1,0:T(8,128)} custom-call(f32[5,4,16,8,128]{4,3,2,1,0:T(8,128)S(1)} %get-tuple-element.12.z_ref, f32[5,4,10,8,128]{4,3,2,1,0:T(8,128)S(1)} %shard_map.20.new_ref, f32[5,4,3,8,128]{4,3,2,1,0:T(8,128)S(1)} %collective-permute-done.2.before_ref, f32[5,4,3,8,128]{4,3,2,1,0:T(8,128)S(1)} %collective-permute-done.3.after_ref), custom_call_target="tpu_custom_call" | custom-call | flops 10000000 | bytes 4194304 | tf_op jit(solution)/shard_map/pallas_call | solution.py:252
Async XLA Ops:
  0.0 1.3 %copy-start = (f32[5,32,16,128]{3,2,1,0:T(8,128)S(1)}, f32[5,32,16,128]{3,2,1,0:T(8,128)}, u32[]{:S(2)}) copy-start(f32[5,32,16,128]{3,2,1,0:T(8,128)} %param.1) | copy-start | bytes 3932164
  1.8 10.9 %collective-permute-start = (f32[5,3,8,128]{3,2,1,0:T(8,128)S(1)}, f32[5,3,8,128]{3,2,1,0:T(8,128)S(1)}, u32[]{:S(2)}, u32[]{:S(2)}) collective-permute-start(f32[5,3,8,128]{3,2,1,0:T(8,128)S(1)} %get-tuple-element.10), channel_id=1, source_target_pairs={{0,32},{32,64},{64,96},{96,128},{128,160},{160,192},{192,224},{224... | collective-permute-start | bytes 184328 | tf_op jit(solution)/shard_map/ppermute | solution.py:237
  8.7 10.3 %collective-permute-start.1 = (f32[5,3,8,128]{3,2,1,0:T(8,128)S(1)}, f32[5,3,8,128]{3,2,1,0:T(8,128)S(1)}, u32[]{:S(2)}, u32[]{:S(2)}) collective-permute-start(f32[5,3,8,128]{3,2,1,0:T(8,128)S(1)} %get-tuple-element.11), channel_id=1, source_target_pairs={{0,224},{32,0},{64,32},{96,64},{128,96},{160,128},{192,160},{224,1... | collective-permute-start | bytes 184328 | tf_op jit(solution)/shard_map/ppermute | solution.py:237
  20.8 9.6 %collective-permute-start.2 = (f32[5,4,3,8,128]{4,3,2,1,0:T(8,128)S(1)}, f32[5,4,3,8,128]{4,3,2,1,0:T(8,128)S(1)}, u32[]{:S(2)}, u32[]{:S(2)}) collective-permute-start(f32[5,4,3,8,128]{4,3,2,1,0:T(8,128)S(1)} %get-tuple-element.13), channel_id=1, source_target_pairs={{0,1},{1,2},{2,3},{3,4},{4,5},{5,6},{6,7},{7,8},{8,9},{9,10},{10,1... | collective-permute-start | bytes 737288 | tf_op jit(solution)/shard_map/ppermute | solution.py:237
  20.9 9.5 %collective-permute-start.3 = (f32[5,4,3,8,128]{4,3,2,1,0:T(8,128)S(1)}, f32[5,4,3,8,128]{4,3,2,1,0:T(8,128)S(1)}, u32[]{:S(2)}, u32[]{:S(2)}) collective-permute-start(f32[5,4,3,8,128]{4,3,2,1,0:T(8,128)S(1)} %get-tuple-element.14), channel_id=1, source_target_pairs={{0,31},{1,0},{2,1},{3,2},{4,3},{5,4},{6,5},{7,6},{8,7},{9,8},{10,9... | collective-permute-start | bytes 737288 | tf_op jit(solution)/shard_map/ppermute | solution.py:237

commit v2 on v1

v2 whole, which is shorter than its diff:
```python
import jax
import jax.numpy as jnp
from jax import lax
from jax.experimental import pallas as pl
from jax.experimental.pallas import tpu as pltpu
from jax.sharding import PartitionSpec as P

adiabatic = 1.4
time_ratio = 0.03
shock_factor = (adiabatic + 1.0) / (2.0 * adiabatic)
floor_share = 0.1
F32 = jnp.float32
SIDE = 3


def reciprocal(values):
    return pl.reciprocal(values, approx=True)


def edges(cells, count):
    far_left, near_left = cells[: count + 3], cells[1 : count + 4]
    near_right, far_right = cells[2 : count + 5], cells[3:]
    face = (7.0 / 12.0) * (near_left + near_right) - (1.0 / 12.0) * (far_left + far_right)
    face = jnp.maximum(face, jnp.minimum(near_left, near_right))
    face = jnp.minimum(face, jnp.maximum(near_left, near_right))
    centre = cells[2 : count + 4]
    left, right = face[: count + 2], face[1:]
    spread = right - left
    below = centre - left
    above = right - centre
    twice_below = below + below
    twice_above = above + above
    monotone = below * above > 0.0
    new_left = jnp.where(
        spread * (below - twice_above) > 0.0,
        centre - jnp.where(monotone, twice_above, 0.0),
        left,
    )
    new_right = jnp.where(
        spread * (twice_below - above) < 0.0,
        centre + jnp.where(monotone, twice_below, 0.0),
        right,
    )
    return new_right[: count + 1], new_left[1:]


def star(dens_left, speed_left, press_left, dens_right, speed_right, press_right):
    scale = adiabatic * shock_factor
    offset = (1.0 - shock_factor) / shock_factor
    scale_left = scale * dens_left
    scale_right = scale * dens_right
    shift_left = offset * press_left
    shift_right = offset * press_right
    jump = speed_left - speed_right
    floor = floor_share * jnp.minimum(press_left, press_right)
    guess = 0.5 * (press_left + press_right)
    for _ in range(5):
        slow_left = lax.rsqrt(scale_left * (guess + shift_left))
        slow_right = lax.rsqrt(scale_right * (guess + shift_right))
        guess = (press_left * slow_left + press_right * slow_right + jump) * reciprocal(
            slow_left + slow_right
        )
        guess = jnp.maximum(guess, floor)
    slow_left = lax.rsqrt(scale_left * (guess + shift_left))
    slow_right = lax.rsqrt(scale_right * (guess + shift_right))
    speed = (
        slow_right * speed_left
        + slow_left * speed_right
        + (press_left - press_right) * (slow_left * slow_right)
    ) * reciprocal(slow_left + slow_right)
    return guess, speed


def advance(cells, count, normal):
    pairs = [edges(c, count) for c in cells]
    left = [p[0] for p in pairs]
    right = [p[1] for p in pairs]
    press_star, speed_star = star(left[0], left[normal], left[4], right[0], right[normal], right[4])
    upwind = speed_star > 0.0
    state = [jnp.where(upwind, a, b) for a, b in zip(left, right)]
    speed = time_ratio * speed_star
    mass = speed * state[0]
    kinetic = 0.5 * (state[1] * state[1] + state[2] * state[2] + state[3] * state[3])
    fluxes = [mass] + [mass * state[i] for i in (1, 2, 3)]
    fluxes[normal] = fluxes[normal] + time_ratio * press_star
    fluxes.append(
        speed * ((1.0 / (adiabatic - 1.0)) * state[4] + press_star) + mass * kinetic
    )
    mid = [c[3 : count + 3] for c in cells]
    change = [f[1:] - f[:-1] for f in fluxes]
    momentum = [mid[0] * mid[i] for i in (1, 2, 3)]
    energy = (1.0 / (adiabatic - 1.0)) * mid[4] + 0.5 * (
        momentum[0] * mid[1] + momentum[1] * mid[2] + momentum[2] * mid[3]
    )
    density = mid[0] - change[0]
    momentum = [m - c for m, c in zip(momentum, change[1:4])]
    energy = energy - change[4]
    thin = reciprocal(density)
    velocity = [m * thin for m in momentum]
    pressure = (adiabatic - 1.0) * (
        energy
        - 0.5 * (momentum[0] * velocity[0] + momentum[1] * velocity[1] + momentum[2] * velocity[2])
    )
    return [density] + velocity + [pressure]


PITCH = 72
LINES = (5, 8 * PITCH, 128)
ROWS = (5, 512, 128)
HALO = (64, 128)
Y_CHUNK = 15


def tile(lines_ref, f, k):
    return lines_ref[f, pl.ds(k, 8, stride=PITCH), :]


def quarter(f, k):
    return pl.ds(4 * (3 * f + k), 4)


def pack_y(x_ref, lines_ref, near_ref, far_ref, rows_ref, sems):
    copies = [pltpu.make_async_copy(x_ref.at[f], rows_ref.at[f], sems.at[f]) for f in range(5)]
    for copy in copies:
        copy.start()
    for f in range(5):
        copies[f].wait()
        for b in range(4):
            turned = rows_ref[f, b * 128 : (b + 1) * 128, :].T
            lines_ref[f, b * PITCH : b * PITCH + 64, :] = turned[:64]
            lines_ref[f, (4 + b) * PITCH : (4 + b) * PITCH + 64, :] = turned[64:]
    odd = lax.rem(lax.axis_index("row"), 2)
    last = 4 * PITCH + 61
    for ref, base in ((near_ref, (1 - odd) * last), (far_ref, odd * last)):
        for f in range(5):
            for k in range(3):
                ref[quarter(f, k), :] = lines_ref[f, pl.ds(base + k, 4, stride=PITCH), :]
        ref[60:64, :] = jnp.zeros((4, 128), F32)


def inner_y(lines_ref, new_ref):
    def step(i, carry):
        at = jnp.minimum(i * Y_CHUNK, 58 - Y_CHUNK)
        cells = [
            jnp.stack([tile(lines_ref, f, at + k) for k in range(Y_CHUNK + 6)]) for f in range(5)
        ]
        out = advance(cells, Y_CHUNK, 2)
        for f in range(5):
            for k in range(Y_CHUNK):
                new_ref[f, pl.ds(at + 3 + k, 8, stride=PITCH), :] = out[f][k]
        return carry

    lax.fori_loop(0, -(-58 // Y_CHUNK), step, 0)


def outer_y(lines_ref, new_ref, near_ref, far_ref, rows_ref, znear_ref, zfar_ref, ext_ref, done_ref):
    even = lax.rem(lax.axis_index("row"), 2) == 0
    near, far = near_ref[...], far_ref[...]
    before, after = jnp.where(even, far, near), jnp.where(even, near, far)
    for f in range(5):
        for k in range(3):
            q = 4 * (3 * f + k)
            ext_ref[f, k, 0:4, :] = before[q : q + 4]
            ext_ref[f, k, 4:8, :] = lines_ref[f, pl.ds(61 + k, 4, stride=PITCH), :]
            ext_ref[f, 3 + k, 0:4, :] = lines_ref[f, pl.ds(4 * PITCH + k, 4, stride=PITCH), :]
            ext_ref[f, 3 + k, 4:8, :] = after[q : q + 4]
    left = [
        jnp.stack([ext_ref[f, k] for k in range(3)] + [tile(lines_ref, f, k) for k in range(6)])
        for f in range(5)
    ]
    right = [
        jnp.stack(
            [tile(lines_ref, f, 58 + k) for k in range(6)] + [ext_ref[f, 3 + k] for k in range(3)]
        )
        for f in range(5)
    ]
    head = advance(left, 3, 2)
    tail = advance(right, 3, 2)
    for f in range(5):
        for m in range(8):
            done_ref[f, m * 64 : (m + 1) * 64, :] = new_ref[f, m * PITCH : m * PITCH + 64, :]
        for k in range(3):
            done_ref[f, pl.ds(k, 8, stride=64), :] = head[f][k]
            done_ref[f, pl.ds(61 + k, 8, stride=64), :] = tail[f][k]
        for b in range(4):
            turned = jnp.concatenate(
                [
                    done_ref[f, b * 64 : (b + 1) * 64, :],
                    done_ref[f, 256 + b * 64 : 256 + (b + 1) * 64, :],
                ]
            )
            rows_ref[f, b * 128 : (b + 1) * 128, :] = turned.T
    odd = lax.rem(lax.axis_index("col"), 2)
    for f in range(5):
        for g in range(4):
            for z in range(3):
                at = 128 * g + z
                znear_ref[f, g, z] = rows_ref[f, pl.ds(at + 13 * (1 - odd), 8, stride=16), :]
                zfar_ref[f, g, z] = rows_ref[f, pl.ds(at + 13 * odd, 8, stride=16), :]


def line_z(rows_ref, f, row, z):
    return rows_ref[f, pl.ds(row + z, 8, stride=16), :]


def inner_z(rows_ref, new_ref):
    def step(g, carry):
        row = pl.multiple_of(128 * g, 128)
        cells = [jnp.stack([line_z(rows_ref, f, row, z) for z in range(16)]) for f in range(5)]
        out = advance(cells, 10, 3)
        for f in range(5):
            new_ref[f, g] = out[f]
        return carry

    lax.fori_loop(0, 4, step, 0)


def outer_z(rows_ref, new_ref, near_ref, far_ref, out_ref, done_ref, sems):
    even = lax.rem(lax.axis_index("col"), 2) == 0
    copies = []
    for g in range(4):
        row = 128 * g
        left, right = [], []
        for f in range(5):
            near, far = near_ref[f, g], far_ref[f, g]
            before, after = jnp.where(even, far, near), jnp.where(even, near, far)
            left.append(
                jnp.concatenate([before, jnp.stack([line_z(rows_ref, f, row, z) for z in range(6)])])
            )
            right.append(
                jnp.concatenate([jnp.stack([line_z(rows_ref, f, row, 10 + z) for z in range(6)]), after])
            )
            for z in range(10):
                done_ref[f, pl.ds(row + 3 + z, 8, stride=16), :] = new_ref[f, g, z]
        for cells, base in ((left, 0), (right, 13)):
            out = advance(cells, 3, 3)
            for f in range(5):
                for z in range(3):
                    done_ref[f, pl.ds(row + base + z, 8, stride=16), :] = out[f][z]
        copies.append(
            pltpu.make_async_copy(
                done_ref.at[:, pl.ds(row, 128)], out_ref.at[:, pl.ds(row, 128)], sems.at[g]
            )
        )
        copies[g].start()
    for copy in copies:
        copy.wait()


def array(*shape):
    return jax.ShapeDtypeStruct(shape, F32)


def kernel(body, outs, scratch=(), sems=0, flops=10**7, outside=None):
    specs = {}
    if outside == "in":
        specs["in_specs"] = [pl.BlockSpec(memory_space=pl.ANY)]
    if outside == "out":
        specs["out_specs"] = pl.BlockSpec(memory_space=pl.ANY)
    scratch = [pltpu.VMEM(s, F32) for s in scratch]
    if sems:
        scratch.append(pltpu.SemaphoreType.DMA((sems,)))
    return pl.pallas_call(
        body,
        out_shape=outs,
        scratch_shapes=scratch,
        compiler_params=pltpu.CompilerParams(vmem_limit_bytes=24 << 20),
        cost_estimate=pl.CostEstimate(flops=flops, bytes_accessed=1 << 22, transcendentals=flops // 20),
        **specs,
    )


def pairs_near(values, axis):
    size = lax.axis_size(axis)
    return lax.ppermute(values, axis, [(i, i ^ 1) for i in range(size)])


def pairs_far(values, axis):
    size = lax.axis_size(axis)
    return lax.ppermute(values, axis, [(i, (i + 1 if i % 2 else i - 1) % size) for i in range(size)])


def on_device(fields):
    x = fields.reshape(ROWS)
    lines, near, far = kernel(
        pack_y, (array(*LINES), array(*HALO), array(*HALO)), [ROWS], 5, outside="in"
    )(x)
    near = pairs_near(near, "row")
    far = pairs_far(far, "row")
    inner = kernel(inner_y, array(*LINES), flops=10**9)(lines)
    edge = array(5, 4, 3, 8, 128)
    rows, near, far = kernel(
        outer_y, (array(*ROWS), edge, edge), [(5, 6, 8, 128), ROWS]
    )(lines, inner, near, far)
    near = pairs_near(near, "col")
    far = pairs_far(far, "col")
    inner = kernel(inner_z, array(5, 4, 10, 8, 128), flops=10**9)(rows)
    out = kernel(outer_z, array(*ROWS), [ROWS], 4, outside="out")(rows, inner, near, far)
    return out.reshape(fields.shape)


def solution(mesh):
    return jax.shard_map(
        on_device,
        mesh=mesh,
        in_specs=(P(None, None, "col", "row"),),
        out_specs=P(None, None, "col", "row"),
        check_vma=False,
    )
```

time: 33.4 us -> 27.7 us (0.83)
  waiting for transfers between devices: 8.2 us -> 1.78 us
  starting transfers between devices: 12.7 us -> 14.9 us
  Pallas kernels: 11.1 us -> 9.32 us
    ppermute x4, waiting for transfers between devices: 8.2 us -> 1.78 us  [the longest x2 1.77 us: pairs_far(): lax.ppermute(values, axis, [(i, (i + 1 if i % 2 else i - 1) % size) for i...]
    ppermute x4, starting transfers between devices: 12.7 us -> 14.9 us  [the longest x2 13.9 us: pairs_far(): lax.ppermute(values, axis, [(i, (i + 1 if i % 2 else i - 1) % size) for i...]
    pallas_call x5, Pallas kernels: 11.1 us -> 9.32 us  [the longest x1 2.89 us: on_device(): inner = kernel(inner_y, array(*LINES), flops=10 ** 9)(lines)]
  transfers between devices with their start and end apart: 4 -> 4, of which waited for: 2 -> 1; matrix products, arithmetic and copies ran while one was open for 0% -> 0% of each run, Pallas kernels for 18% -> 18%
where the time goes in v2:
time: 27.7 us; the launch traced here: 27.3 us
  starting transfers between devices  14.9 us (54%)
  Pallas kernels  9.32 us (34%)
  waiting for transfers between devices  1.78 us (6%)
  local copies, waits for them, and re-layouts  1.32 us (5%)
    ppermute x2, starting transfers between devices, pairs_far(): lax.ppermute(values, axis, [(i, (i + 1 if i % 2 else i - 1) % size) for i...  13.9 us
    pallas_call x1, Pallas kernels, on_device(): inner = kernel(inner_y, array(*LINES), flops=10 ** 9)(lines)  2.89 us
    pallas_call x1, Pallas kernels, on_device(): kernel(outer_z, array(*ROWS), [ROWS], 4, outside='out')  2.62 us
    pallas_call x1, Pallas kernels, on_device(): inner = kernel(inner_z, array(5, 4, 10, 8, 128), flops=10 ** 9)(rows)  2.09 us
    ppermute x2, waiting for transfers between devices, pairs_far(): lax.ppermute(values, axis, [(i, (i + 1 if i % 2 else i - 1) % size) for i...  1.77 us
    unnamed x2, local copies, waits for them, and re-layouts  1.32 us
    ppermute x2, starting transfers between devices, pairs_near(): return lax.ppermute(values, axis, [(i, i ^ 1) for i in range(size)])  0.92 us
    pallas_call x1, Pallas kernels, on_device(): kernel(outer_y, (array(*ROWS), edge, edge), [(5, 6, 8, 128), ROWS])  0.9 us
  transfers between devices with their start and end apart: 4, of which 1 were waited for; matrix products, arithmetic and copies ran while one was open for 0% of the time, Pallas kernels for 18%

profile of v2, /device:TPU:24, one launch (start us, length us, event | category | flops | bytes accessed | tf_op | source)
XLA Modules:
  0.0 27.3 jit_solution(17910993794999659489)
XLA Ops:
  0.0 0.0 copy-start
  0.0 1.3 %copy-done = f32[5,32,16,128]{3,2,1,0:T(8,128)S(1)} copy-done((f32[5,32,16,128]{3,2,1,0:T(8,128)S(1)}, f32[5,32,16,128]{3,2,1,0:T(8,128)}, u32[]{:S(2)}) %copy-start) | copy-done | bytes 1310744
  1.3 0.8 %shard_map.17 = (f32[5,576,128]{2,1,0:T(8,128)S(1)}, f32[64,128]{1,0:T(8,128)S(1)}, f32[64,128]{1,0:T(8,128)S(1)}) custom-call(f32[5,512,128]{2,1,0:T(8,128)S(1)} %bitcast.2), custom_call_target="tpu_custom_call" | custom-call | flops 10000000 | bytes 4194304 | tf_op jit(solution)/shard_map/pallas_call | solution.py:285
  2.1 0.8 %collective-permute-start = (f32[64,128]{1,0:T(8,128)S(1)}, f32[64,128]{1,0:T(8,128)S(1)}, u32[]{:S(2)}, u32[]{:S(2)}) collective-permute-start(f32[64,128]{1,0:T(8,128)S(1)} %get-tuple-element.12), channel_id=1, source_target_pairs={{0,32},{32,0},{64,96},{96,64},{128,160},{160,128},{192,224},{224,1... | collective-permute-start | bytes 98312 | tf_op jit(solution)/shard_map/ppermute | solution.py:275
  3.0 7.7 %collective-permute-start.1 = (f32[64,128]{1,0:T(8,128)S(1)}, f32[64,128]{1,0:T(8,128)S(1)}, u32[]{:S(2)}, u32[]{:S(2)}) collective-permute-start(f32[64,128]{1,0:T(8,128)S(1)} %get-tuple-element.13), channel_id=1, source_target_pairs={{0,224},{32,64},{64,32},{96,128},{128,96},{160,192},{192,160},{224... | collective-permute-start | bytes 98312 | tf_op jit(solution)/shard_map/ppermute | solution.py:280
  10.7 2.9 %shard_map.18.new_ref = f32[5,576,128]{2,1,0:T(8,128)S(1)} custom-call(f32[5,576,128]{2,1,0:T(8,128)S(1)} %get-tuple-element.11.lines_ref), custom_call_target="tpu_custom_call" | custom-call | flops 1000000000 | bytes 4194304 | tf_op jit(solution)/shard_map/pallas_call | solution.py:290
  13.6 0.0 collective-permute-done.near_ref
  13.6 0.0 collective-permute-done.1.far_ref
  13.6 0.9 %shard_map.19 = (f32[5,512,128]{2,1,0:T(8,128)S(1)}, f32[5,4,3,8,128]{4,3,2,1,0:T(8,128)S(1)}, f32[5,4,3,8,128]{4,3,2,1,0:T(8,128)S(1)}) custom-call(f32[5,576,128]{2,1,0:T(8,128)S(1)} %get-tuple-element.11.lines_ref, f32[5,576,128]{2,1,0:T(8,128)S(1)} %shard_map.18.new_ref, f32[64,128]{1,0:T(8,128)S(1)} %collective-permute-done.near_ref, ...), custom_call_target="tpu_custom_call" | custom-call | flops 10000000 | bytes 4194304 | tf_op jit(solution)/shard_map/pallas_call | solution.py:292
  14.5 0.1 collective-permute-start.2
  14.6 6.3 %collective-permute-start.3 = (f32[5,4,3,8,128]{4,3,2,1,0:T(8,128)S(1)}, f32[5,4,3,8,128]{4,3,2,1,0:T(8,128)S(1)}, u32[]{:S(2)}, u32[]{:S(2)}) collective-permute-start(f32[5,4,3,8,128]{4,3,2,1,0:T(8,128)S(1)} %get-tuple-element.16), channel_id=1, source_target_pairs={{0,31},{1,2},{2,1},{3,4},{4,3},{5,6},{6,5},{7,8},{8,7},{9,10},{10,... | collective-permute-start | bytes 737288 | tf_op jit(solution)/shard_map/ppermute | solution.py:280
  20.8 2.1 %shard_map.20.new_ref = f32[5,4,10,8,128]{4,3,2,1,0:T(8,128)S(1)} custom-call(f32[5,512,128]{2,1,0:T(8,128)S(1)} %get-tuple-element.14.rows_ref), custom_call_target="tpu_custom_call" | custom-call | flops 1000000000 | bytes 4194304 | tf_op jit(solution)/shard_map/pallas_call | solution.py:297
  22.9 0.0 collective-permute-done.2.near_ref
  22.9 1.8 %collective-permute-done.3.far_ref = f32[5,4,3,8,128]{4,3,2,1,0:T(8,128)S(1)} collective-permute-done((f32[5,4,3,8,128]{4,3,2,1,0:T(8,128)S(1)}, f32[5,4,3,8,128]{4,3,2,1,0:T(8,128)S(1)}, u32[]{:S(2)}, u32[]{:S(2)}) %collective-permute-start.3) | collective-permute-done | bytes 245792 | tf_op jit(solution)/shard_map/ppermute | solution.py:280
  24.7 2.6 %shard_map.21 = f32[5,512,128]{2,1,0:T(8,128)} custom-call(f32[5,512,128]{2,1,0:T(8,128)S(1)} %get-tuple-element.14.rows_ref, f32[5,4,10,8,128]{4,3,2,1,0:T(8,128)S(1)} %shard_map.20.new_ref, f32[5,4,3,8,128]{4,3,2,1,0:T(8,128)S(1)} %collective-permute-done.2.near_ref, f32[5,4,3,8,128]{4,3,2,1,0:T(8,128)S(1)} %collective-permute-done.3.far_ref), custom_call_target="tpu_custom_call" | custom-call | flops 10000000 | bytes 4194304 | tf_op jit(solution)/shard_map/pallas_call | solution.py:298
Async XLA Ops:
  0.0 1.3 %copy-start = (f32[5,32,16,128]{3,2,1,0:T(8,128)S(1)}, f32[5,32,16,128]{3,2,1,0:T(8,128)}, u32[]{:S(2)}) copy-start(f32[5,32,16,128]{3,2,1,0:T(8,128)} %param.1) | copy-start | bytes 3932164
  2.1 11.4 %collective-permute-start = (f32[64,128]{1,0:T(8,128)S(1)}, f32[64,128]{1,0:T(8,128)S(1)}, u32[]{:S(2)}, u32[]{:S(2)}) collective-permute-start(f32[64,128]{1,0:T(8,128)S(1)} %get-tuple-element.12), channel_id=1, source_target_pairs={{0,32},{32,0},{64,96},{96,64},{128,160},{160,128},{192,224},{224,1... | collective-permute-start | bytes 98312 | tf_op jit(solution)/shard_map/ppermute | solution.py:275
  3.0 10.6 %collective-permute-start.1 = (f32[64,128]{1,0:T(8,128)S(1)}, f32[64,128]{1,0:T(8,128)S(1)}, u32[]{:S(2)}, u32[]{:S(2)}) collective-permute-start(f32[64,128]{1,0:T(8,128)S(1)} %get-tuple-element.13), channel_id=1, source_target_pairs={{0,224},{32,64},{64,32},{96,128},{128,96},{160,192},{192,160},{224... | collective-permute-start | bytes 98312 | tf_op jit(solution)/shard_map/ppermute | solution.py:280
  14.5 8.5 %collective-permute-start.2 = (f32[5,4,3,8,128]{4,3,2,1,0:T(8,128)S(1)}, f32[5,4,3,8,128]{4,3,2,1,0:T(8,128)S(1)}, u32[]{:S(2)}, u32[]{:S(2)}) collective-permute-start(f32[5,4,3,8,128]{4,3,2,1,0:T(8,128)S(1)} %get-tuple-element.15), channel_id=1, source_target_pairs={{0,1},{1,0},{2,3},{3,2},{4,5},{5,4},{6,7},{7,6},{8,9},{9,8},{10,11... | collective-permute-start | bytes 737288 | tf_op jit(solution)/shard_map/ppermute | solution.py:275
  14.6 10.1 %collective-permute-start.3 = (f32[5,4,3,8,128]{4,3,2,1,0:T(8,128)S(1)}, f32[5,4,3,8,128]{4,3,2,1,0:T(8,128)S(1)}, u32[]{:S(2)}, u32[]{:S(2)}) collective-permute-start(f32[5,4,3,8,128]{4,3,2,1,0:T(8,128)S(1)} %get-tuple-element.16), channel_id=1, source_target_pairs={{0,31},{1,2},{2,1},{3,4},{4,3},{5,6},{6,5},{7,8},{8,7},{9,10},{10,... | collective-permute-start | bytes 737288 | tf_op jit(solution)/shard_map/ppermute | solution.py:280

commit v3 on v2

--- a/solution.py
+++ b/solution.py
@@ -1,3 +1,5 @@
+import functools
+
 import jax
 import jax.numpy as jnp
 from jax import lax
@@ -41,7 +43,7 @@
         centre + jnp.where(monotone, twice_below, 0.0),
         right,
     )
-    return new_right[: count + 1], new_left[1:]
+    return new_left, new_right
 
 
 def star(dens_left, speed_left, press_left, dens_right, speed_right, press_right):
@@ -71,10 +73,7 @@
     return guess, speed
 
 
-def advance(cells, count, normal):
-    pairs = [edges(c, count) for c in cells]
-    left = [p[0] for p in pairs]
-    right = [p[1] for p in pairs]
+def flux(left, right, normal):
     press_star, speed_star = star(left[0], left[normal], left[4], right[0], right[normal], right[4])
     upwind = speed_star > 0.0
     state = [jnp.where(upwind, a, b) for a, b in zip(left, right)]
@@ -83,11 +82,11 @@
     kinetic = 0.5 * (state[1] * state[1] + state[2] * state[2] + state[3] * state[3])
     fluxes = [mass] + [mass * state[i] for i in (1, 2, 3)]
     fluxes[normal] = fluxes[normal] + time_ratio * press_star
-    fluxes.append(
-        speed * ((1.0 / (adiabatic - 1.0)) * state[4] + press_star) + mass * kinetic
-    )
-    mid = [c[3 : count + 3] for c in cells]
-    change = [f[1:] - f[:-1] for f in fluxes]
+    fluxes.append(speed * ((1.0 / (adiabatic - 1.0)) * state[4] + press_star) + mass * kinetic)
+    return fluxes
+
+
+def update(mid, change):
     momentum = [mid[0] * mid[i] for i in (1, 2, 3)]
     energy = (1.0 / (adiabatic - 1.0)) * mid[4] + 0.5 * (
         momentum[0] * mid[1] + momentum[1] * mid[2] + momentum[2] * mid[3]
@@ -104,11 +103,38 @@
     return [density] + velocity + [pressure]
 
 
+def inner(cells, count, normal):
+    pairs = [edges(c, count) for c in cells]
+    left = [p[1][: count + 1] for p in pairs]
+    right = [p[0][1:] for p in pairs]
+    fluxes = flux(left, right, normal)
+    new = update([c[3 : count + 3] for c in cells], [f[1:] - f[:-1] for f in fluxes])
+    low = [p[0][0] for p in pairs], [f[0] for f in fluxes]
+    high = [p[1][count + 1] for p in pairs], [f[count] for f in fluxes]
+    return new, low, high
+
+
+def outer_low(cells, low, normal):
+    pairs = [edges(c, 2) for c in cells]
+    left = [p[1][:3] for p in pairs]
+    right = [jnp.concatenate([p[0][1:3], edge[None]]) for p, edge in zip(pairs, low[0])]
+    fluxes = [jnp.concatenate([a, b[None]]) for a, b in zip(flux(left, right, normal), low[1])]
+    return update([c[3:6] for c in cells], [f[1:] - f[:-1] for f in fluxes])
+
+
+def outer_high(cells, high, normal):
+    pairs = [edges(c, 2) for c in cells]
+    left = [jnp.concatenate([edge[None], p[1][1:3]]) for p, edge in zip(pairs, high[0])]
+    right = [p[0][1:] for p in pairs]
+    fluxes = [jnp.concatenate([b[None], a]) for a, b in zip(flux(left, right, normal), high[1])]
+    return update([c[2:5] for c in cells], [f[1:] - f[:-1] for f in fluxes])
+
+
 PITCH = 72
 LINES = (5, 8 * PITCH, 128)
 ROWS = (5, 512, 128)
 HALO = (64, 128)
-Y_CHUNK = 15
+Y_CHUNK = 29
 
 
 def tile(lines_ref, f, k):
@@ -123,37 +149,47 @@
     copies = [pltpu.make_async_copy(x_ref.at[f], rows_ref.at[f], sems.at[f]) for f in range(5)]
     for copy in copies:
         copy.start()
+    odd = lax.rem(lax.axis_index("row"), 2)
+    last = 4 * PITCH + 61
     for f in range(5):
         copies[f].wait()
         for b in range(4):
             turned = rows_ref[f, b * 128 : (b + 1) * 128, :].T
             lines_ref[f, b * PITCH : b * PITCH + 64, :] = turned[:64]
             lines_ref[f, (4 + b) * PITCH : (4 + b) * PITCH + 64, :] = turned[64:]
-    odd = lax.rem(lax.axis_index("row"), 2)
-    last = 4 * PITCH + 61
-    for ref, base in ((near_ref, (1 - odd) * last), (far_ref, odd * last)):
-        for f in range(5):
+        for ref, base in ((near_ref, (1 - odd) * last), (far_ref, odd * last)):
             for k in range(3):
                 ref[quarter(f, k), :] = lines_ref[f, pl.ds(base + k, 4, stride=PITCH), :]
+    for ref in (near_ref, far_ref):
         ref[60:64, :] = jnp.zeros((4, 128), F32)
 
 
-def inner_y(lines_ref, new_ref):
-    def step(i, carry):
-        at = jnp.minimum(i * Y_CHUNK, 58 - Y_CHUNK)
+def keep(rim_ref, which, end):
+    for i in range(2):
+        for f in range(5):
+            rim_ref[which, i, f] = end[i][f]
+
+
+def kept(rim_ref, which):
+    return [[rim_ref[which, i, f] for f in range(5)] for i in range(2)]
+
+
+def inner_y(lines_ref, new_ref, rim_ref):
+    for at in range(0, 58, Y_CHUNK):
         cells = [
             jnp.stack([tile(lines_ref, f, at + k) for k in range(Y_CHUNK + 6)]) for f in range(5)
         ]
-        out = advance(cells, Y_CHUNK, 2)
+        new, low, high = inner(cells, Y_CHUNK, 2)
+        if at == 0:
+            keep(rim_ref, 0, low)
+        if at + Y_CHUNK == 58:
+            keep(rim_ref, 1, high)
         for f in range(5):
             for k in range(Y_CHUNK):
-                new_ref[f, pl.ds(at + 3 + k, 8, stride=PITCH), :] = out[f][k]
-        return carry
-
-    lax.fori_loop(0, -(-58 // Y_CHUNK), step, 0)
-
-
-def outer_y(lines_ref, new_ref, near_ref, far_ref, rows_ref, znear_ref, zfar_ref, ext_ref, done_ref):
+                new_ref[f, pl.ds(at + 3 + k, 8, stride=PITCH), :] = new[f][k]
+
+
+def outer_y(lines_ref, new_ref, rim_ref, near_ref, far_ref, rows_ref, znear_ref, zfar_ref, ext_ref, done_ref):
     even = lax.rem(lax.axis_index("row"), 2) == 0
     near, far = near_ref[...], far_ref[...]
     before, after = jnp.where(even, far, near), jnp.where(even, near, far)
@@ -164,18 +200,18 @@
             ext_ref[f, k, 4:8, :] = lines_ref[f, pl.ds(61 + k, 4, stride=PITCH), :]
             ext_ref[f, 3 + k, 0:4, :] = lines_ref[f, pl.ds(4 * PITCH + k, 4, stride=PITCH), :]
             ext_ref[f, 3 + k, 4:8, :] = after[q : q + 4]
-    left = [
-        jnp.stack([ext_ref[f, k] for k in range(3)] + [tile(lines_ref, f, k) for k in range(6)])
+    below = [
+        jnp.stack([ext_ref[f, k] for k in range(3)] + [tile(lines_ref, f, k) for k in range(5)])
         for f in range(5)
     ]
-    right = [
+    above = [
         jnp.stack(
-            [tile(lines_ref, f, 58 + k) for k in range(6)] + [ext_ref[f, 3 + k] for k in range(3)]
+            [tile(lines_ref, f, 59 + k) for k in range(5)] + [ext_ref[f, 3 + k] for k in range(3)]
         )
         for f in range(5)
     ]
-    head = advance(left, 3, 2)
-    tail = advance(right, 3, 2)
+    head = outer_low(below, kept(rim_ref, 0), 2)
+    tail = outer_high(above, kept(rim_ref, 1), 2)
     for f in range(5):
         for m in range(8):
             done_ref[f, m * 64 : (m + 1) * 64, :] = new_ref[f, m * PITCH : m * PITCH + 64, :]
@@ -191,52 +227,60 @@
             )
             rows_ref[f, b * 128 : (b + 1) * 128, :] = turned.T
     odd = lax.rem(lax.axis_index("col"), 2)
+    message_z(rows_ref, znear_ref, 13 - 13 * odd)
+    message_z(rows_ref, zfar_ref, 13 * odd)
+
+
+def message_z(rows_ref, message_ref, base):
     for f in range(5):
         for g in range(4):
             for z in range(3):
-                at = 128 * g + z
-                znear_ref[f, g, z] = rows_ref[f, pl.ds(at + 13 * (1 - odd), 8, stride=16), :]
-                zfar_ref[f, g, z] = rows_ref[f, pl.ds(at + 13 * odd, 8, stride=16), :]
+                message_ref[f, g, z] = rows_ref[f, pl.ds(128 * g + z + base, 8, stride=16), :]
 
 
 def line_z(rows_ref, f, row, z):
     return rows_ref[f, pl.ds(row + z, 8, stride=16), :]
 
 
-def inner_z(rows_ref, new_ref):
+def inner_z(rows_ref, new_ref, rim_ref, *, start):
     def step(g, carry):
-        row = pl.multiple_of(128 * g, 128)
+        row = pl.multiple_of(128 * (start + g), 128)
         cells = [jnp.stack([line_z(rows_ref, f, row, z) for z in range(16)]) for f in range(5)]
-        out = advance(cells, 10, 3)
+        new, low, high = inner(cells, 10, 3)
+        keep(rim_ref, 2 * g, low)
+        keep(rim_ref, 2 * g + 1, high)
         for f in range(5):
-            new_ref[f, g] = out[f]
+            new_ref[f, g] = new[f]
         return carry
 
-    lax.fori_loop(0, 4, step, 0)
-
-
-def outer_z(rows_ref, new_ref, near_ref, far_ref, out_ref, done_ref, sems):
+    lax.fori_loop(0, 2, step, 0)
+
+
+def outer_z(rows_ref, one_ref, rim_one_ref, two_ref, rim_two_ref, near_ref, far_ref, out_ref, done_ref, sems):
     even = lax.rem(lax.axis_index("col"), 2) == 0
     copies = []
     for g in range(4):
         row = 128 * g
-        left, right = [], []
+        new_ref, rim_ref = ((one_ref, rim_one_ref), (two_ref, rim_two_ref))[g // 2]
+        h = g % 2
+        below, above = [], []
         for f in range(5):
             near, far = near_ref[f, g], far_ref[f, g]
             before, after = jnp.where(even, far, near), jnp.where(even, near, far)
-            left.append(
-                jnp.concatenate([before, jnp.stack([line_z(rows_ref, f, row, z) for z in range(6)])])
+            below.append(
+                jnp.concatenate([before, jnp.stack([line_z(rows_ref, f, row, z) for z in range(5)])])
             )
-            right.append(
-                jnp.concatenate([jnp.stack([line_z(rows_ref, f, row, 10 + z) for z in range(6)]), after])
+            above.append(
+                jnp.concatenate([jnp.stack([line_z(rows_ref, f, row, 11 + z) for z in range(5)]), after])
             )
             for z in range(10):
-                done_ref[f, pl.ds(row + 3 + z, 8, stride=16), :] = new_ref[f, g, z]
-        for cells, base in ((left, 0), (right, 13)):
-            out = advance(cells, 3, 3)
+                done_ref[f, pl.ds(row + 3 + z, 8, stride=16), :] = new_ref[f, h, z]
+        head = outer_low(below, kept(rim_ref, 2 * h), 3)
+        tail = outer_high(above, kept(rim_ref, 2 * h + 1), 3)
+        for cells, base in ((head, 0), (tail, 13)):
             for f in range(5):
                 for z in range(3):
-                    done_ref[f, pl.ds(row + base + z, 8, stride=16), :] = out[f][z]
+                    done_ref[f, pl.ds(row + base + z, 8, stride=16), :] = cells[f][z]
         copies.append(
             pltpu.make_async_copy(
                 done_ref.at[:, pl.ds(row, 128)], out_ref.at[:, pl.ds(row, 128)], sems.at[g]
@@ -251,12 +295,12 @@
     return jax.ShapeDtypeStruct(shape, F32)
 
 
-def kernel(body, outs, scratch=(), sems=0, flops=10**7, outside=None):
+def kernel(body, outs, scratch=(), sems=0, flops=10**7, outside=None, room=24):
     specs = {}
     if outside == "in":
-        specs["in_specs"] = [pl.BlockSpec(memory_space=pl.ANY)]
+        specs["in_specs"] = [pl.BlockSpec(memory_space=pltpu.HBM)]
     if outside == "out":
-        specs["out_specs"] = pl.BlockSpec(memory_space=pl.ANY)
+        specs["out_specs"] = pl.BlockSpec(memory_space=pltpu.HBM)
     scratch = [pltpu.VMEM(s, F32) for s in scratch]
     if sems:
         scratch.append(pltpu.SemaphoreType.DMA((sems,)))
@@ -264,7 +308,7 @@
         body,
         out_shape=outs,
         scratch_shapes=scratch,
-        compiler_params=pltpu.CompilerParams(vmem_limit_bytes=24 << 20),
+        compiler_params=pltpu.CompilerParams(vmem_limit_bytes=room << 20),
         cost_estimate=pl.CostEstimate(flops=flops, bytes_accessed=1 << 22, transcendentals=flops // 20),
         **specs,
     )
@@ -281,21 +325,24 @@
 
 
 def on_device(fields):
-    x = fields.reshape(ROWS)
+    x = pltpu.with_memory_space_constraint(fields.reshape(ROWS), pltpu.HBM)
     lines, near, far = kernel(
         pack_y, (array(*LINES), array(*HALO), array(*HALO)), [ROWS], 5, outside="in"
     )(x)
     near = pairs_near(near, "row")
     far = pairs_far(far, "row")
-    inner = kernel(inner_y, array(*LINES), flops=10**9)(lines)
-    edge = array(5, 4, 3, 8, 128)
-    rows, near, far = kernel(
-        outer_y, (array(*ROWS), edge, edge), [(5, 6, 8, 128), ROWS]
-    )(lines, inner, near, far)
+    new, rim = kernel(inner_y, (array(*LINES), array(2, 2, 5, 8, 128)), flops=10**9)(lines)
+    message = array(5, 4, 3, 8, 128)
+    rows, near, far = kernel(outer_y, (array(*ROWS), message, message), [(5, 6, 8, 128), ROWS])(
+        lines, new, rim, near, far
+    )
+    far = pairs_far(far, "col")
+    half = (array(5, 2, 10, 8, 128), array(4, 2, 5, 8, 128))
+    one = kernel(functools.partial(inner_z, start=0), half, flops=10**9)(rows)
+    one, rows, near = lax.optimization_barrier((one, rows, near))
     near = pairs_near(near, "col")
-    far = pairs_far(far, "col")
-    inner = kernel(inner_z, array(5, 4, 10, 8, 128), flops=10**9)(rows)
-    out = kernel(outer_z, array(*ROWS), [ROWS], 4, outside="out")(rows, inner, near, far)
+    two = kernel(functools.partial(inner_z, start=2), half, flops=10**9)(rows)
+    out = kernel(outer_z, array(*ROWS), [ROWS], 4, outside="out")(rows, *one, *two, near, far)
     return out.reshape(fields.shape)
 
 

time: 27.7 us -> 26.1 us (0.942)
  starting transfers between devices: 14.9 us -> 13.1 us
  local copies, waits for them, and re-layouts: 1.32 us -> 0 us
  waiting for transfers between devices: 1.78 us -> 2.91 us
    ppermute x2, starting transfers between devices: 13.9 us -> 12.2 us  [pairs_far(): lax.ppermute(values, axis, [(i, (i + 1 if i % 2 else i - 1) % size) for i...]
    unnamed x2 -> x0, local copies, waits for them, and re-layouts: 1.32 us -> none
    ppermute x2, waiting for transfers between devices: 1.77 us -> 2.9 us  [pairs_far(): lax.ppermute(values, axis, [(i, (i + 1 if i % 2 else i - 1) % size) for i...]
    pallas_call x1, Pallas kernels: 0.82 us -> 1.7 us  [on_device(): kernel(pack_y, (array(*LINES), array(*HALO), array(*HALO)), [ROWS], 5, ou...]
    pallas_call x1, Pallas kernels: 2.62 us -> 2.23 us  [on_device(): kernel(outer_z, array(*ROWS), [ROWS], 4, outside='out')]
    pallas_call x3 -> x4, Pallas kernels: 5.88 us -> 5.6 us  [the longest x1 2.65 us: on_device(): kernel(inner_y, (array(*LINES), array(2, 2, 5, 8, 128)), flops=10 ** 9)]
  transfers between devices with their start and end apart: 4 -> 4, of which waited for: 1 -> 1; matrix products, arithmetic and copies ran while one was open for 0% -> 0% of each run, Pallas kernels for 18% -> 19%
where the time goes in v3:
time: 26.1 us; the launch traced here: 25.6 us
  starting transfers between devices  13.1 us (50%)
  Pallas kernels  9.52 us (36%)
  waiting for transfers between devices  2.91 us (11%)
    ppermute x2, starting transfers between devices, pairs_far(): lax.ppermute(values, axis, [(i, (i + 1 if i % 2 else i - 1) % size) for i...  12.2 us
    ppermute x2, waiting for transfers between devices, pairs_far(): lax.ppermute(values, axis, [(i, (i + 1 if i % 2 else i - 1) % size) for i...  2.9 us
    pallas_call x1, Pallas kernels, on_device(): kernel(inner_y, (array(*LINES), array(2, 2, 5, 8, 128)), flops=10 ** 9)  2.65 us
    pallas_call x1, Pallas kernels, on_device(): kernel(outer_z, array(*ROWS), [ROWS], 4, outside='out')  2.23 us
    pallas_call x1, Pallas kernels, on_device(): kernel(pack_y, (array(*LINES), array(*HALO), array(*HALO)), [ROWS], 5, ou...  1.7 us
    pallas_call x1, Pallas kernels, on_device(): two = kernel(functools.partial(inner_z, start=2), half, flops=10 ** 9)(rows)  1.06 us
    pallas_call x1, Pallas kernels, on_device(): one = kernel(functools.partial(inner_z, start=0), half, flops=10 ** 9)(rows)  1.06 us
    ppermute x2, starting transfers between devices, pairs_near(): return lax.ppermute(values, axis, [(i, i ^ 1) for i in range(size)])  0.93 us
  transfers between devices with their start and end apart: 4, of which 1 were waited for; matrix products, arithmetic and copies ran while one was open for 0% of the time, Pallas kernels for 19%

profile of v3, /device:TPU:24, one launch (start us, length us, event | category | flops | bytes accessed | tf_op | source)
XLA Modules:
  0.0 25.6 jit_solution(15807107506600826525)
XLA Ops:
  0.0 1.7 %shard_map.17 = (f32[5,576,128]{2,1,0:T(8,128)S(1)}, f32[64,128]{1,0:T(8,128)S(1)}, f32[64,128]{1,0:T(8,128)S(1)}) custom-call(f32[5,512,128]{2,1,0:T(8,128)} %bitcast.2), custom_call_target="tpu_custom_call" | custom-call | flops 10000000 | bytes 4194304 | tf_op jit(solution)/shard_map/pallas_call | solution.py:329
  1.7 0.8 %collective-permute-start = (f32[64,128]{1,0:T(8,128)S(1)}, f32[64,128]{1,0:T(8,128)S(1)}, u32[]{:S(2)}, u32[]{:S(2)}) collective-permute-start(f32[64,128]{1,0:T(8,128)S(1)} %get-tuple-element.24), channel_id=1, source_target_pairs={{0,32},{32,0},{64,96},{96,64},{128,160},{160,128},{192,224},{224,1... | collective-permute-start | bytes 98312 | tf_op jit(solution)/shard_map/ppermute | solution.py:319
  2.5 7.7 %collective-permute-start.1 = (f32[64,128]{1,0:T(8,128)S(1)}, f32[64,128]{1,0:T(8,128)S(1)}, u32[]{:S(2)}, u32[]{:S(2)}) collective-permute-start(f32[64,128]{1,0:T(8,128)S(1)} %get-tuple-element.25), channel_id=1, source_target_pairs={{0,224},{32,64},{64,32},{96,128},{128,96},{160,192},{192,160},{224... | collective-permute-start | bytes 98312 | tf_op jit(solution)/shard_map/ppermute | solution.py:324
  10.2 2.6 %shard_map.18 = (f32[5,576,128]{2,1,0:T(8,128)S(1)}, f32[2,2,5,8,128]{4,3,2,1,0:T(8,128)S(1)}) custom-call(f32[5,576,128]{2,1,0:T(8,128)S(1)} %get-tuple-element.21.lines_ref), custom_call_target="tpu_custom_call" | custom-call | flops 1000000000 | bytes 4194304 | tf_op jit(solution)/shard_map/pallas_call | solution.py:334
  12.9 0.0 collective-permute-done.near_ref
  12.9 0.0 collective-permute-done.1.far_ref
  12.9 0.8 %shard_map.19 = (f32[5,512,128]{2,1,0:T(8,128)S(1)}, f32[5,4,3,8,128]{4,3,2,1,0:T(8,128)S(1)}, f32[5,4,3,8,128]{4,3,2,1,0:T(8,128)S(1)}) custom-call(f32[5,576,128]{2,1,0:T(8,128)S(1)} %get-tuple-element.21.lines_ref, f32[5,576,128]{2,1,0:T(8,128)S(1)} %get-tuple-element.22.new_ref, f32[2,2,5,8,128]{4,3,2,1,0:T(8,128)S(1)} %get-tuple-element.23.rim_ref, ...), custom_call_target="tpu_custom_call" | custom-call | flops 10000000 | bytes 4194304 | tf_op jit(solution)/shard_map/pallas_call | solution.py:336
  13.7 4.5 %collective-permute-start.3 = (f32[5,4,3,8,128]{4,3,2,1,0:T(8,128)S(1)}, f32[5,4,3,8,128]{4,3,2,1,0:T(8,128)S(1)}, u32[]{:S(2)}, u32[]{:S(2)}) collective-permute-start(f32[5,4,3,8,128]{4,3,2,1,0:T(8,128)S(1)} %get-tuple-element.36), channel_id=1, source_target_pairs={{0,31},{1,2},{2,1},{3,4},{4,3},{5,6},{6,5},{7,8},{8,7},{9,10},{10,... | collective-permute-start | bytes 737288 | tf_op jit(solution)/shard_map/ppermute | solution.py:324
  18.2 1.1 %shard_map.20 = (f32[5,2,10,8,128]{4,3,2,1,0:T(8,128)S(1)}, f32[4,2,5,8,128]{4,3,2,1,0:T(8,128)S(1)}) custom-call(f32[5,512,128]{2,1,0:T(8,128)S(1)} %get-tuple-element.30.rows_ref), custom_call_target="tpu_custom_call" | custom-call | flops 1000000000 | bytes 4194304 | tf_op jit(solution)/shard_map/pallas_call | solution.py:341
  19.3 0.1 collective-permute-start.2
  19.4 1.1 %shard_map.21 = (f32[5,2,10,8,128]{4,3,2,1,0:T(8,128)S(1)}, f32[4,2,5,8,128]{4,3,2,1,0:T(8,128)S(1)}) custom-call(f32[5,512,128]{2,1,0:T(8,128)S(1)} %get-tuple-element.30.rows_ref), custom_call_target="tpu_custom_call" | custom-call | flops 1000000000 | bytes 4194304 | tf_op jit(solution)/shard_map/pallas_call | solution.py:344
  20.4 2.9 %collective-permute-done.3.far_ref = f32[5,4,3,8,128]{4,3,2,1,0:T(8,128)S(1)} collective-permute-done((f32[5,4,3,8,128]{4,3,2,1,0:T(8,128)S(1)}, f32[5,4,3,8,128]{4,3,2,1,0:T(8,128)S(1)}, u32[]{:S(2)}, u32[]{:S(2)}) %collective-permute-start.3) | collective-permute-done | bytes 245792 | tf_op jit(solution)/shard_map/ppermute | solution.py:324
  23.3 0.0 collective-permute-done.2.near_ref
  23.3 2.2 %shard_map.22 = f32[5,512,128]{2,1,0:T(8,128)} custom-call(f32[5,512,128]{2,1,0:T(8,128)S(1)} %get-tuple-element.30.rows_ref, f32[5,2,10,8,128]{4,3,2,1,0:T(8,128)S(1)} %get-tuple-element.31.one_ref, f32[4,2,5,8,128]{4,3,2,1,0:T(8,128)S(1)} %get-tuple-element.32.rim_one_ref, f32[5,2,10,8,128]{4,3,2,1,0:T(8,128)S(1)} %get-tuple-element.33.two_ref, ...), custom_call_target="tpu_custom_call" | custom-call | flops 10000000 | bytes 4194304 | tf_op jit(solution)/shard_map/pallas_call | solution.py:345
Async XLA Ops:
  1.7 11.2 %collective-permute-start = (f32[64,128]{1,0:T(8,128)S(1)}, f32[64,128]{1,0:T(8,128)S(1)}, u32[]{:S(2)}, u32[]{:S(2)}) collective-permute-start(f32[64,128]{1,0:T(8,128)S(1)} %get-tuple-element.24), channel_id=1, source_target_pairs={{0,32},{32,0},{64,96},{96,64},{128,160},{160,128},{192,224},{224,1... | collective-permute-start | bytes 98312 | tf_op jit(solution)/shard_map/ppermute | solution.py:319
  2.5 10.3 %collective-permute-start.1 = (f32[64,128]{1,0:T(8,128)S(1)}, f32[64,128]{1,0:T(8,128)S(1)}, u32[]{:S(2)}, u32[]{:S(2)}) collective-permute-start(f32[64,128]{1,0:T(8,128)S(1)} %get-tuple-element.25), channel_id=1, source_target_pairs={{0,224},{32,64},{64,32},{96,128},{128,96},{160,192},{192,160},{224... | collective-permute-start | bytes 98312 | tf_op jit(solution)/shard_map/ppermute | solution.py:324
  13.7 9.6 %collective-permute-start.3 = (f32[5,4,3,8,128]{4,3,2,1,0:T(8,128)S(1)}, f32[5,4,3,8,128]{4,3,2,1,0:T(8,128)S(1)}, u32[]{:S(2)}, u32[]{:S(2)}) collective-permute-start(f32[5,4,3,8,128]{4,3,2,1,0:T(8,128)S(1)} %get-tuple-element.36), channel_id=1, source_target_pairs={{0,31},{1,2},{2,1},{3,4},{4,3},{5,6},{6,5},{7,8},{8,7},{9,10},{10,... | collective-permute-start | bytes 737288 | tf_op jit(solution)/shard_map/ppermute | solution.py:324
  19.3 4.1 %collective-permute-start.2 = (f32[5,4,3,8,128]{4,3,2,1,0:T(8,128)S(1)}, f32[5,4,3,8,128]{4,3,2,1,0:T(8,128)S(1)}, u32[]{:S(2)}, u32[]{:S(2)}) collective-permute-start(f32[5,4,3,8,128]{4,3,2,1,0:T(8,128)S(1)} %get-tuple-element.35), channel_id=1, source_target_pairs={{0,1},{1,0},{2,3},{3,2},{4,5},{5,4},{6,7},{7,6},{8,9},{9,8},{10,11... | collective-permute-start | bytes 737288 | tf_op jit(solution)/shard_map/ppermute | solution.py:319

commit v4 on v3

--- a/solution.py
+++ b/solution.py
@@ -130,6 +130,7 @@
     return update([c[2:5] for c in cells], [f[1:] - f[:-1] for f in fluxes])
 
 
+PAD = 61
 PITCH = 72
 LINES = (5, 8 * PITCH, 128)
 ROWS = (5, 512, 128)
@@ -145,7 +146,7 @@
     return pl.ds(4 * (3 * f + k), 4)
 
 
-def pack_y(x_ref, lines_ref, near_ref, far_ref, rows_ref, sems):
+def pack_y(x_ref, lines_ref, near_ref, far_ref, again_ref, rows_ref, sems):
     copies = [pltpu.make_async_copy(x_ref.at[f], rows_ref.at[f], sems.at[f]) for f in range(5)]
     for copy in copies:
         copy.start()
@@ -157,10 +158,10 @@
             turned = rows_ref[f, b * 128 : (b + 1) * 128, :].T
             lines_ref[f, b * PITCH : b * PITCH + 64, :] = turned[:64]
             lines_ref[f, (4 + b) * PITCH : (4 + b) * PITCH + 64, :] = turned[64:]
-        for ref, base in ((near_ref, (1 - odd) * last), (far_ref, odd * last)):
+        for ref, base in ((near_ref, (1 - odd) * last), (far_ref, odd * last), (again_ref, (1 - odd) * last)):
             for k in range(3):
                 ref[quarter(f, k), :] = lines_ref[f, pl.ds(base + k, 4, stride=PITCH), :]
-    for ref in (near_ref, far_ref):
+    for ref in (near_ref, far_ref, again_ref):
         ref[60:64, :] = jnp.zeros((4, 128), F32)
 
 
@@ -189,9 +190,10 @@
                 new_ref[f, pl.ds(at + 3 + k, 8, stride=PITCH), :] = new[f][k]
 
 
-def outer_y(lines_ref, new_ref, rim_ref, near_ref, far_ref, rows_ref, znear_ref, zfar_ref, ext_ref, done_ref):
+def outer_y(lines_ref, new_ref, rim_ref, first_ref, far_ref, second_ref, rows_ref, znear_ref, zfar_ref, ext_ref, rim_rows_ref):
     even = lax.rem(lax.axis_index("row"), 2) == 0
-    near, far = near_ref[...], far_ref[...]
+    near = jnp.where(lax.axis_index("row") < 4, first_ref[...], second_ref[...])
+    far = far_ref[...]
     before, after = jnp.where(even, far, near), jnp.where(even, near, far)
     for f in range(5):
         for k in range(3):
@@ -212,19 +214,21 @@
     ]
     head = outer_low(below, kept(rim_ref, 0), 2)
     tail = outer_high(above, kept(rim_ref, 1), 2)
+    row = lax.broadcasted_iota(jnp.int32, (8, 128), 0)
     for f in range(5):
+        for k in range(3):
+            rim_rows_ref[f, pl.ds(k, 8, stride=16), :] = head[f][k]
+            rim_rows_ref[f, pl.ds(13 + k, 8, stride=16), :] = tail[f][k]
+        runs = []
         for m in range(8):
-            done_ref[f, m * 64 : (m + 1) * 64, :] = new_ref[f, m * PITCH : m * PITCH + 64, :]
-        for k in range(3):
-            done_ref[f, pl.ds(k, 8, stride=64), :] = head[f][k]
-            done_ref[f, pl.ds(61 + k, 8, stride=64), :] = tail[f][k]
+            at = m * PITCH
+            first = jnp.where(row < 3, rim_rows_ref[f, 16 * m : 16 * m + 8, :], new_ref[f, at : at + 8, :])
+            last = jnp.where(
+                row < 5, new_ref[f, at + 56 : at + 64, :], rim_rows_ref[f, 16 * m + 8 : 16 * m + 16, :]
+            )
+            runs.append([first, new_ref[f, at + 8 : at + 56, :], last])
         for b in range(4):
-            turned = jnp.concatenate(
-                [
-                    done_ref[f, b * 64 : (b + 1) * 64, :],
-                    done_ref[f, 256 + b * 64 : 256 + (b + 1) * 64, :],
-                ]
-            )
+            turned = jnp.concatenate(runs[b] + runs[4 + b])
             rows_ref[f, b * 128 : (b + 1) * 128, :] = turned.T
     odd = lax.rem(lax.axis_index("col"), 2)
     message_z(rows_ref, znear_ref, 13 - 13 * odd)
@@ -235,16 +239,16 @@
     for f in range(5):
         for g in range(4):
             for z in range(3):
-                message_ref[f, g, z] = rows_ref[f, pl.ds(128 * g + z + base, 8, stride=16), :]
+                message_ref[(4 * f + g) * 3 + z] = rows_ref[f, pl.ds(128 * g + z + base, 8, stride=16), :]
 
 
 def line_z(rows_ref, f, row, z):
     return rows_ref[f, pl.ds(row + z, 8, stride=16), :]
 
 
-def inner_z(rows_ref, new_ref, rim_ref, *, start):
+def inner_z(rows_ref, new_ref, rim_ref):
     def step(g, carry):
-        row = pl.multiple_of(128 * (start + g), 128)
+        row = pl.multiple_of(128 * g, 128)
         cells = [jnp.stack([line_z(rows_ref, f, row, z) for z in range(16)]) for f in range(5)]
         new, low, high = inner(cells, 10, 3)
         keep(rim_ref, 2 * g, low)
@@ -253,37 +257,30 @@
             new_ref[f, g] = new[f]
         return carry
 
-    lax.fori_loop(0, 2, step, 0)
-
-
-def outer_z(rows_ref, one_ref, rim_one_ref, two_ref, rim_two_ref, near_ref, far_ref, out_ref, done_ref, sems):
-    even = lax.rem(lax.axis_index("col"), 2) == 0
+    lax.fori_loop(0, 4, step, 0)
+
+
+def finish(side, rows_ref, new_ref, rim_ref, halo_ref, out_ref, half_ref, sems):
+    flat_ref, blocks_ref = half_ref, half_ref.reshape(5, 32, 8, 128)
     copies = []
     for g in range(4):
         row = 128 * g
-        new_ref, rim_ref = ((one_ref, rim_one_ref), (two_ref, rim_two_ref))[g // 2]
-        h = g % 2
-        below, above = [], []
-        for f in range(5):
-            near, far = near_ref[f, g], far_ref[f, g]
-            before, after = jnp.where(even, far, near), jnp.where(even, near, far)
-            below.append(
-                jnp.concatenate([before, jnp.stack([line_z(rows_ref, f, row, z) for z in range(5)])])
-            )
-            above.append(
-                jnp.concatenate([jnp.stack([line_z(rows_ref, f, row, 11 + z) for z in range(5)]), after])
-            )
-            for z in range(10):
-                done_ref[f, pl.ds(row + 3 + z, 8, stride=16), :] = new_ref[f, h, z]
-        head = outer_low(below, kept(rim_ref, 2 * h), 3)
-        tail = outer_high(above, kept(rim_ref, 2 * h + 1), 3)
-        for cells, base in ((head, 0), (tail, 13)):
-            for f in range(5):
-                for z in range(3):
-                    done_ref[f, pl.ds(row + base + z, 8, stride=16), :] = cells[f][z]
+        cells = []
+        for f in range(5):
+            own = jnp.stack([line_z(rows_ref, f, row, (0, 11)[side] + z) for z in range(5)])
+            pair = (halo_ref[pl.ds((4 * f + g) * 3, 3)], own) if side == 0 else (own, halo_ref[pl.ds((4 * f + g) * 3, 3)])
+            cells.append(jnp.concatenate(pair))
+        edge = (outer_low, outer_high)[side](cells, kept(rim_ref, 2 * g + side), 3)
+        for f in range(5):
+            for z in range(3):
+                flat_ref[f, pl.ds(64 * g + (0, 5)[side] + z, 8, stride=8), :] = edge[f][z]
+            for z in range(5):
+                flat_ref[f, pl.ds(64 * g + (3, 0)[side] + z, 8, stride=8), :] = new_ref[
+                    f, g, (0, 5)[side] + z
+                ]
         copies.append(
             pltpu.make_async_copy(
-                done_ref.at[:, pl.ds(row, 128)], out_ref.at[:, pl.ds(row, 128)], sems.at[g]
+                blocks_ref.at[:, pl.ds(8 * g, 8)], out_ref.at[:, pl.ds(8 * g, 8), side], sems.at[g]
             )
         )
         copies[g].start()
@@ -291,16 +288,37 @@
         copy.wait()
 
 
+def either_side(is_low, *refs):
+    for side in (0, 1):
+
+        @pl.when(is_low if side == 0 else jnp.logical_not(is_low))
+        def _():
+            finish(side, *refs)
+
+
+def near_z(rows_ref, new_ref, rim_ref, halo_ref, out_ref, half_ref, sems):
+    either_side(lax.rem(lax.axis_index("col"), 2) == 1, rows_ref, new_ref, rim_ref, halo_ref, out_ref, half_ref, sems)
+
+
+def far_z(rows_ref, new_ref, rim_ref, halo_ref, part_ref, out_ref, half_ref, sems):
+    del part_ref
+    either_side(lax.rem(lax.axis_index("col"), 2) == 0, rows_ref, new_ref, rim_ref, halo_ref, out_ref, half_ref, sems)
+
+
 def array(*shape):
     return jax.ShapeDtypeStruct(shape, F32)
 
 
-def kernel(body, outs, scratch=(), sems=0, flops=10**7, outside=None, room=24):
+def kernel(body, outs, scratch=(), sems=0, flops=10**7, outside=None, room=24, carried=None, moved=1 << 22):
     specs = {}
     if outside == "in":
         specs["in_specs"] = [pl.BlockSpec(memory_space=pltpu.HBM)]
     if outside == "out":
         specs["out_specs"] = pl.BlockSpec(memory_space=pltpu.HBM)
+    if carried is not None:
+        vmem, hbm = pl.BlockSpec(memory_space=pltpu.VMEM), pl.BlockSpec(memory_space=pltpu.HBM)
+        specs["in_specs"] = [vmem] * carried + [hbm]
+        specs["input_output_aliases"] = {carried: 0}
     scratch = [pltpu.VMEM(s, F32) for s in scratch]
     if sems:
         scratch.append(pltpu.SemaphoreType.DMA((sems,)))
@@ -309,7 +327,7 @@
         out_shape=outs,
         scratch_shapes=scratch,
         compiler_params=pltpu.CompilerParams(vmem_limit_bytes=room << 20),
-        cost_estimate=pl.CostEstimate(flops=flops, bytes_accessed=1 << 22, transcendentals=flops // 20),
+        cost_estimate=pl.CostEstimate(flops=flops, bytes_accessed=moved, transcendentals=flops // 20),
         **specs,
     )
 
@@ -319,6 +337,16 @@
     return lax.ppermute(values, axis, [(i, i ^ 1) for i in range(size)])
 
 
+def near_rows(values, start):
+    columns = lax.axis_size("col")
+    steps = []
+    for row in range(8):
+        for col in range(columns):
+            to = (row ^ 1, col) if start <= row < start + 4 else (row, col ^ 1)
+            steps.append((row * columns + col, to[0] * columns + to[1]))
+    return lax.ppermute(values, ("row", "col"), steps)
+
+
 def pairs_far(values, axis):
     size = lax.axis_size(axis)
     return lax.ppermute(values, axis, [(i, (i + 1 if i % 2 else i - 1) % size) for i in range(size)])
@@ -326,23 +354,23 @@
 
 def on_device(fields):
     x = pltpu.with_memory_space_constraint(fields.reshape(ROWS), pltpu.HBM)
-    lines, near, far = kernel(
-        pack_y, (array(*LINES), array(*HALO), array(*HALO)), [ROWS], 5, outside="in"
+    lines, near, far, again = kernel(
+        pack_y, (array(*LINES), array(*HALO), array(*HALO), array(*HALO)), [ROWS], 5, outside="in"
     )(x)
-    near = pairs_near(near, "row")
+    first = near_rows(near, 0)
     far = pairs_far(far, "row")
+    second = near_rows(again, 4)
     new, rim = kernel(inner_y, (array(*LINES), array(2, 2, 5, 8, 128)), flops=10**9)(lines)
-    message = array(5, 4, 3, 8, 128)
-    rows, near, far = kernel(outer_y, (array(*ROWS), message, message), [(5, 6, 8, 128), ROWS])(
-        lines, new, rim, near, far
+    rows, near, far = kernel(outer_y, (array(*ROWS), array(60, 8, 128), array(PAD, 8, 128)), [(5, 6, 8, 128), (5, 128, 128)])(
+        lines, new, rim, first, far, second
     )
     far = pairs_far(far, "col")
-    half = (array(5, 2, 10, 8, 128), array(4, 2, 5, 8, 128))
-    one = kernel(functools.partial(inner_z, start=0), half, flops=10**9)(rows)
-    one, rows, near = lax.optimization_barrier((one, rows, near))
     near = pairs_near(near, "col")
-    two = kernel(functools.partial(inner_z, start=2), half, flops=10**9)(rows)
-    out = kernel(outer_z, array(*ROWS), [ROWS], 4, outside="out")(rows, *one, *two, near, far)
+    new, rim = kernel(inner_z, (array(5, 4, 10, 8, 128), array(8, 2, 5, 8, 128)), flops=1000000000, moved=4194304)(rows)
+    split = array(5, 32, 2, 8, 128)
+    half = [(5, 256, 128)]
+    part = kernel(near_z, split, half, 4, outside="out", flops=10000000, moved=1048576)(rows, new, rim, near)
+    out = kernel(far_z, split, half, 4, outside="out", carried=4)(rows, new, rim, far, part)
     return out.reshape(fields.shape)
 
 

time: 26.1 us -> 26 us (level)
  the two profiles are of different devices: /device:TPU:24 before, /device:TPU:1 now
where the time goes in v4:
time: 26 us; the launch traced here: 25.9 us
  starting transfers between devices  15.6 us (60%)
  Pallas kernels  10.2 us (39%)
    ppermute x2, starting transfers between devices, pairs_far(): lax.ppermute(values, axis, [(i, (i + 1 if i % 2 else i - 1) % size) for i...  10.1 us
    ppermute x1, starting transfers between devices, pairs_near(): return lax.ppermute(values, axis, [(i, i ^ 1) for i in range(size)])  2.98 us
    pallas_call x1, Pallas kernels, on_device(): kernel(inner_y, (array(*LINES), array(2, 2, 5, 8, 128)), flops=10 ** 9)  2.65 us
    ppermute x2, starting transfers between devices, near_rows(): return lax.ppermute(values, ('row', 'col'), steps)  2.57 us
    pallas_call x1, Pallas kernels, on_device(): kernel(inner_z, (array(5, 4, 10, 8, 128), array(8, 2, 5, 8, 128)), flops=...  2.12 us
    pallas_call x1, Pallas kernels, on_device(): kernel(pack_y, (array(*LINES), array(*HALO), array(*HALO), array(*HALO)),...  1.71 us
    pallas_call x1, Pallas kernels, on_device(): kernel(far_z, split, half, 4, outside='out', carried=4)  1.47 us
    pallas_call x1, Pallas kernels, on_device(): kernel(near_z, split, half, 4, outside='out', flops=10000000, moved=1048576)  1.42 us
  transfers between devices with their start and end apart: 5, of which 0 were waited for; matrix products, arithmetic and copies ran while one was open for 0% of the time, Pallas kernels for 24%

profile of v4, /device:TPU:1, one launch (start us, length us, event | category | flops | bytes accessed | tf_op | source)
XLA Modules:
  0.0 25.9 jit_solution(5014442255275183556)
XLA Ops:
  0.0 1.7 %shard_map.17 = (f32[5,576,128]{2,1,0:T(8,128)S(1)}, f32[64,128]{1,0:T(8,128)S(1)}, f32[64,128]{1,0:T(8,128)S(1)}, f32[64,128]{1,0:T(8,128)S(1)}) custom-call(f32[5,512,128]{2,1,0:T(8,128)} %bitcast.2), custom_call_target="tpu_custom_call" | custom-call | flops 10000000 | bytes 4194304 | tf_op jit(solution)/shard_map/pallas_call | solution.py:357
  1.7 2.2 %collective-permute-start = (f32[64,128]{1,0:T(8,128)S(1)}, f32[64,128]{1,0:T(8,128)S(1)}, u32[]{:S(2)}, u32[]{:S(2)}) collective-permute-start(f32[64,128]{1,0:T(8,128)S(1)} %get-tuple-element.19), channel_id=1, source_target_pairs={{0,32},{1,33},{2,34},{3,35},{4,36},{5,37},{6,38},{7,39},{8,40},{9,... | collective-permute-start | bytes 98312 | tf_op jit(solution)/shard_map/ppermute | solution.py:347
  3.9 8.8 %collective-permute-start.1 = (f32[64,128]{1,0:T(8,128)S(1)}, f32[64,128]{1,0:T(8,128)S(1)}, u32[]{:S(2)}, u32[]{:S(2)}) collective-permute-start(f32[64,128]{1,0:T(8,128)S(1)} %get-tuple-element.20), channel_id=1, source_target_pairs={{0,224},{32,64},{64,32},{96,128},{128,96},{160,192},{192,160},{224... | collective-permute-start | bytes 98312 | tf_op jit(solution)/shard_map/ppermute | solution.py:352
  12.7 0.4 %collective-permute-start.2 = (f32[64,128]{1,0:T(8,128)S(1)}, f32[64,128]{1,0:T(8,128)S(1)}, u32[]{:S(2)}, u32[]{:S(2)}) collective-permute-start(f32[64,128]{1,0:T(8,128)S(1)} %get-tuple-element.21), channel_id=1, source_target_pairs={{0,1},{1,0},{2,3},{3,2},{4,5},{5,4},{6,7},{7,6},{8,9},{9,8},{10,11... | collective-permute-start | bytes 98312 | tf_op jit(solution)/shard_map/ppermute | solution.py:347
  13.0 2.6 %shard_map.18 = (f32[5,576,128]{2,1,0:T(8,128)S(1)}, f32[2,2,5,8,128]{4,3,2,1,0:T(8,128)S(1)}) custom-call(f32[5,576,128]{2,1,0:T(8,128)S(1)} %get-tuple-element.16.lines_ref), custom_call_target="tpu_custom_call" | custom-call | flops 1000000000 | bytes 4194304 | tf_op jit(solution)/shard_map/pallas_call | solution.py:363
  15.7 0.0 collective-permute-done.first_ref
  15.7 0.0 collective-permute-done.1.far_ref
  15.7 0.0 collective-permute-done.2.second_ref
  15.7 0.8 %shard_map.19 = (f32[5,512,128]{2,1,0:T(8,128)S(1)}, f32[60,8,128]{2,1,0:T(8,128)S(1)}, f32[61,8,128]{2,1,0:T(8,128)S(1)}) custom-call(f32[5,576,128]{2,1,0:T(8,128)S(1)} %get-tuple-element.16.lines_ref, f32[5,576,128]{2,1,0:T(8,128)S(1)} %get-tuple-element.17.new_ref, f32[2,2,5,8,128]{4,3,2,1,0:T(8,128)S(1)} %get-tuple-element.18.rim_ref, ...), custom_call_target="tpu_custom_call" | custom-call | flops 10000000 | bytes 4194304 | tf_op jit(solution)/shard_map/pallas_call | solution.py:364
  16.5 1.3 %collective-permute-start.3 = (f32[61,8,128]{2,1,0:T(8,128)S(1)}, f32[61,8,128]{2,1,0:T(8,128)S(1)}, u32[]{:S(2)}, u32[]{:S(2)}) collective-permute-start(f32[61,8,128]{2,1,0:T(8,128)S(1)} %get-tuple-element.25), channel_id=1, source_target_pairs={{0,31},{1,2},{2,1},{3,4},{4,3},{5,6},{6,5},{7,8},{8,7},{9,10},{10,... | collective-permute-start | bytes 749576 | tf_op jit(solution)/shard_map/ppermute | solution.py:352
  17.9 3.0 %collective-permute-start.4 = (f32[60,8,128]{2,1,0:T(8,128)S(1)}, f32[60,8,128]{2,1,0:T(8,128)S(1)}, u32[]{:S(2)}, u32[]{:S(2)}) collective-permute-start(f32[60,8,128]{2,1,0:T(8,128)S(1)} %get-tuple-element.26), channel_id=1, source_target_pairs={{0,1},{1,0},{2,3},{3,2},{4,5},{5,4},{6,7},{7,6},{8,9},{9,8},{10,11... | collective-permute-start | bytes 737288 | tf_op jit(solution)/shard_map/ppermute | solution.py:337
  20.8 2.1 %shard_map.20 = (f32[5,4,10,8,128]{4,3,2,1,0:T(8,128)S(1)}, f32[8,2,5,8,128]{4,3,2,1,0:T(8,128)S(1)}) custom-call(f32[5,512,128]{2,1,0:T(8,128)S(1)} %get-tuple-element.22.rows_ref), custom_call_target="tpu_custom_call" | custom-call | flops 1000000000 | bytes 4194304 | tf_op jit(solution)/shard_map/pallas_call | solution.py:369
  23.0 0.0 collective-permute-done.4.halo_ref
  23.0 1.4 %shard_map.21.part_ref = f32[5,32,2,8,128]{4,3,2,1,0:T(8,128)} custom-call(f32[5,512,128]{2,1,0:T(8,128)S(1)} %get-tuple-element.22.rows_ref, f32[5,4,10,8,128]{4,3,2,1,0:T(8,128)S(1)} %get-tuple-element.23.new_ref, f32[8,2,5,8,128]{4,3,2,1,0:T(8,128)S(1)} %get-tuple-element.24.rim_ref, f32[60,8,128]{2,1,0:T(8,128)S(1)} %collective-permute-done.4.halo_ref), custom_call_target="tpu_custom_call" | custom-call | flops 10000000 | bytes 1048576 | tf_op jit(solution)/shard_map/pallas_call | solution.py:372
  24.4 0.0 collective-permute-done.3.halo_ref
  24.4 1.5 %shard_map.22 = f32[5,32,2,8,128]{4,3,2,1,0:T(8,128)} custom-call(f32[5,512,128]{2,1,0:T(8,128)S(1)} %get-tuple-element.22.rows_ref, f32[5,4,10,8,128]{4,3,2,1,0:T(8,128)S(1)} %get-tuple-element.23.new_ref, f32[8,2,5,8,128]{4,3,2,1,0:T(8,128)S(1)} %get-tuple-element.24.rim_ref, ...), custom_call_target="tpu_custom_call", output_to_operand_aliasing={{}: (4, {})} | custom-call | flops 10000000 | bytes 4194304 | tf_op jit(solution)/shard_map/pallas_call | solution.py:373
Async XLA Ops:
  1.7 14.0 %collective-permute-start = (f32[64,128]{1,0:T(8,128)S(1)}, f32[64,128]{1,0:T(8,128)S(1)}, u32[]{:S(2)}, u32[]{:S(2)}) collective-permute-start(f32[64,128]{1,0:T(8,128)S(1)} %get-tuple-element.19), channel_id=1, source_target_pairs={{0,32},{1,33},{2,34},{3,35},{4,36},{5,37},{6,38},{7,39},{8,40},{9,... | collective-permute-start | bytes 98312 | tf_op jit(solution)/shard_map/ppermute | solution.py:347
  3.9 11.8 %collective-permute-start.1 = (f32[64,128]{1,0:T(8,128)S(1)}, f32[64,128]{1,0:T(8,128)S(1)}, u32[]{:S(2)}, u32[]{:S(2)}) collective-permute-start(f32[64,128]{1,0:T(8,128)S(1)} %get-tuple-element.20), channel_id=1, source_target_pairs={{0,224},{32,64},{64,32},{96,128},{128,96},{160,192},{192,160},{224... | collective-permute-start | bytes 98312 | tf_op jit(solution)/shard_map/ppermute | solution.py:352
  12.7 3.0 %collective-permute-start.2 = (f32[64,128]{1,0:T(8,128)S(1)}, f32[64,128]{1,0:T(8,128)S(1)}, u32[]{:S(2)}, u32[]{:S(2)}) collective-permute-start(f32[64,128]{1,0:T(8,128)S(1)} %get-tuple-element.21), channel_id=1, source_target_pairs={{0,1},{1,0},{2,3},{3,2},{4,5},{5,4},{6,7},{7,6},{8,9},{9,8},{10,11... | collective-permute-start | bytes 98312 | tf_op jit(solution)/shard_map/ppermute | solution.py:347
  16.5 7.9 %collective-permute-start.3 = (f32[61,8,128]{2,1,0:T(8,128)S(1)}, f32[61,8,128]{2,1,0:T(8,128)S(1)}, u32[]{:S(2)}, u32[]{:S(2)}) collective-permute-start(f32[61,8,128]{2,1,0:T(8,128)S(1)} %get-tuple-element.25), channel_id=1, source_target_pairs={{0,31},{1,2},{2,1},{3,4},{4,3},{5,6},{6,5},{7,8},{8,7},{9,10},{10,... | collective-permute-start | bytes 749576 | tf_op jit(solution)/shard_map/ppermute | solution.py:352
  17.9 5.1 %collective-permute-start.4 = (f32[60,8,128]{2,1,0:T(8,128)S(1)}, f32[60,8,128]{2,1,0:T(8,128)S(1)}, u32[]{:S(2)}, u32[]{:S(2)}) collective-permute-start(f32[60,8,128]{2,1,0:T(8,128)S(1)} %get-tuple-element.26), channel_id=1, source_target_pairs={{0,1},{1,0},{2,3},{3,2},{4,5},{5,4},{6,7},{7,6},{8,9},{9,8},{10,11... | collective-permute-start | bytes 737288 | tf_op jit(solution)/shard_map/ppermute | solution.py:337

commit v5 on v4

--- a/solution.py
+++ b/solution.py
@@ -246,7 +246,7 @@
     return rows_ref[f, pl.ds(row + z, 8, stride=16), :]
 
 
-def inner_z(rows_ref, new_ref, rim_ref):
+def inner_z(rows_ref, new_ref, rim_ref, *, odd):
     def step(g, carry):
         row = pl.multiple_of(128 * g, 128)
         cells = [jnp.stack([line_z(rows_ref, f, row, z) for z in range(16)]) for f in range(5)]
@@ -257,23 +257,27 @@
             new_ref[f, g] = new[f]
         return carry
 
-    lax.fori_loop(0, 4, step, 0)
+    @pl.when(lax.rem(lax.axis_index("col"), 2) == odd)
+    def _():
+        lax.fori_loop(0, 4, step, 0)
 
 
 def finish(side, rows_ref, new_ref, rim_ref, halo_ref, out_ref, half_ref, sems):
     flat_ref, blocks_ref = half_ref, half_ref.reshape(5, 32, 8, 128)
-    copies = []
+    sides = []
     for g in range(4):
         row = 128 * g
         cells = []
         for f in range(5):
             own = jnp.stack([line_z(rows_ref, f, row, (0, 11)[side] + z) for z in range(5)])
-            pair = (halo_ref[pl.ds((4 * f + g) * 3, 3)], own) if side == 0 else (own, halo_ref[pl.ds((4 * f + g) * 3, 3)])
-            cells.append(jnp.concatenate(pair))
-        edge = (outer_low, outer_high)[side](cells, kept(rim_ref, 2 * g + side), 3)
+            halo = halo_ref[pl.ds((4 * f + g) * 3, 3)]
+            cells.append(jnp.concatenate((halo, own) if side == 0 else (own, halo)))
+        sides.append((outer_low, outer_high)[side](cells, kept(rim_ref, 2 * g + side), 3))
+    copies = []
+    for g in range(4):
         for f in range(5):
             for z in range(3):
-                flat_ref[f, pl.ds(64 * g + (0, 5)[side] + z, 8, stride=8), :] = edge[f][z]
+                flat_ref[f, pl.ds(64 * g + (0, 5)[side] + z, 8, stride=8), :] = sides[g][f][z]
             for z in range(5):
                 flat_ref[f, pl.ds(64 * g + (3, 0)[side] + z, 8, stride=8), :] = new_ref[
                     f, g, (0, 5)[side] + z
@@ -288,21 +292,29 @@
         copy.wait()
 
 
-def either_side(is_low, *refs):
-    for side in (0, 1):
-
-        @pl.when(is_low if side == 0 else jnp.logical_not(is_low))
-        def _():
-            finish(side, *refs)
-
-
-def near_z(rows_ref, new_ref, rim_ref, halo_ref, out_ref, half_ref, sems):
-    either_side(lax.rem(lax.axis_index("col"), 2) == 1, rows_ref, new_ref, rim_ref, halo_ref, out_ref, half_ref, sems)
-
-
-def far_z(rows_ref, new_ref, rim_ref, halo_ref, part_ref, out_ref, half_ref, sems):
+def near_z(rows_ref, odd_ref, odd_rim_ref, even_ref, even_rim_ref, halo_ref, *refs):
+    odd = lax.rem(lax.axis_index("col"), 2) == 1
+
+    @pl.when(odd)
+    def _():
+        finish(0, rows_ref, odd_ref, odd_rim_ref, halo_ref, *refs)
+
+    @pl.when(jnp.logical_not(odd))
+    def _():
+        finish(1, rows_ref, even_ref, even_rim_ref, halo_ref, *refs)
+
+
+def far_z(rows_ref, odd_ref, odd_rim_ref, even_ref, even_rim_ref, halo_ref, part_ref, *refs):
     del part_ref
-    either_side(lax.rem(lax.axis_index("col"), 2) == 0, rows_ref, new_ref, rim_ref, halo_ref, out_ref, half_ref, sems)
+    odd = lax.rem(lax.axis_index("col"), 2) == 1
+
+    @pl.when(odd)
+    def _():
+        finish(1, rows_ref, odd_ref, odd_rim_ref, halo_ref, *refs)
+
+    @pl.when(jnp.logical_not(odd))
+    def _():
+        finish(0, rows_ref, even_ref, even_rim_ref, halo_ref, *refs)
 
 
 def array(*shape):
@@ -365,12 +377,15 @@
         lines, new, rim, first, far, second
     )
     far = pairs_far(far, "col")
+    inner_cells = (array(5, 4, 10, 8, 128), array(8, 2, 5, 8, 128))
+    odd = kernel(functools.partial(inner_z, odd=1), inner_cells, flops=1000000000, moved=4194304)(rows)
+    odd, rows, near = lax.optimization_barrier((odd, rows, near))
     near = pairs_near(near, "col")
-    new, rim = kernel(inner_z, (array(5, 4, 10, 8, 128), array(8, 2, 5, 8, 128)), flops=1000000000, moved=4194304)(rows)
+    even = kernel(functools.partial(inner_z, odd=0), inner_cells, flops=1000000000, moved=4194304)(rows)
     split = array(5, 32, 2, 8, 128)
     half = [(5, 256, 128)]
-    part = kernel(near_z, split, half, 4, outside="out", flops=10000000, moved=1048576)(rows, new, rim, near)
-    out = kernel(far_z, split, half, 4, outside="out", carried=4)(rows, new, rim, far, part)
+    part = kernel(near_z, split, half, 4, outside="out", flops=10000000, moved=1048576)(rows, *odd, *even, near)
+    out = kernel(far_z, split, half, 4, outside="out", carried=6)(rows, *odd, *even, far, part)
     return out.reshape(fields.shape)
 
 

time: 26 us -> 25.1 us (0.965)
  the two profiles are of different devices: /device:TPU:1 before, /device:TPU:7 now
where the time goes in v5:
time: 25.1 us; the launch traced here: 25 us
  starting transfers between devices  11.4 us (45%)
  Pallas kernels  10.2 us (41%)
  waiting for transfers between devices  3.4 us (14%)
    ppermute x2, starting transfers between devices, pairs_far(): lax.ppermute(values, axis, [(i, (i + 1 if i % 2 else i - 1) % size) for i...  9.52 us
    pallas_call x1, Pallas kernels, on_device(): kernel(inner_y, (array(*LINES), array(2, 2, 5, 8, 128)), flops=10 ** 9)  2.65 us
    pallas_call x1, Pallas kernels, on_device(): kernel(functools.partial(inner_z, odd=1), inner_cells, flops=1000000000,...  2.15 us
    ppermute x2, waiting for transfers between devices, pairs_far(): lax.ppermute(values, axis, [(i, (i + 1 if i % 2 else i - 1) % size) for i...  1.92 us
    ppermute x2, starting transfers between devices, near_rows(): return lax.ppermute(values, ('row', 'col'), steps)  1.74 us
    pallas_call x1, Pallas kernels, on_device(): kernel(pack_y, (array(*LINES), array(*HALO), array(*HALO), array(*HALO)),...  1.71 us
    ppermute x1, waiting for transfers between devices, pairs_near(): return lax.ppermute(values, axis, [(i, i ^ 1) for i in range(size)])  1.47 us
    pallas_call x1, Pallas kernels, on_device(): kernel(far_z, split, half, 4, outside='out', carried=6)  1.43 us
  transfers between devices with their start and end apart: 5, of which 2 were waited for; matrix products, arithmetic and copies ran while one was open for 0% of the time, Pallas kernels for 25%

profile of v5, /device:TPU:7, one launch (start us, length us, event | category | flops | bytes accessed | tf_op | source)
XLA Modules:
  0.0 25.0 jit_solution(10275831276915103067)
XLA Ops:
  0.0 1.7 %shard_map.17 = (f32[5,576,128]{2,1,0:T(8,128)S(1)}, f32[64,128]{1,0:T(8,128)S(1)}, f32[64,128]{1,0:T(8,128)S(1)}, f32[64,128]{1,0:T(8,128)S(1)}) custom-call(f32[5,512,128]{2,1,0:T(8,128)} %bitcast.2), custom_call_target="tpu_custom_call" | custom-call | flops 10000000 | bytes 4194304 | tf_op jit(solution)/shard_map/pallas_call | solution.py:369
  1.7 1.4 %collective-permute-start = (f32[64,128]{1,0:T(8,128)S(1)}, f32[64,128]{1,0:T(8,128)S(1)}, u32[]{:S(2)}, u32[]{:S(2)}) collective-permute-start(f32[64,128]{1,0:T(8,128)S(1)} %get-tuple-element.25), channel_id=1, source_target_pairs={{0,32},{1,33},{2,34},{3,35},{4,36},{5,37},{6,38},{7,39},{8,40},{9,... | collective-permute-start | bytes 98312 | tf_op jit(solution)/shard_map/ppermute | solution.py:359
  3.1 8.8 %collective-permute-start.1 = (f32[64,128]{1,0:T(8,128)S(1)}, f32[64,128]{1,0:T(8,128)S(1)}, u32[]{:S(2)}, u32[]{:S(2)}) collective-permute-start(f32[64,128]{1,0:T(8,128)S(1)} %get-tuple-element.26), channel_id=1, source_target_pairs={{0,224},{32,64},{64,32},{96,128},{128,96},{160,192},{192,160},{224... | collective-permute-start | bytes 98312 | tf_op jit(solution)/shard_map/ppermute | solution.py:364
  11.9 0.4 %collective-permute-start.2 = (f32[64,128]{1,0:T(8,128)S(1)}, f32[64,128]{1,0:T(8,128)S(1)}, u32[]{:S(2)}, u32[]{:S(2)}) collective-permute-start(f32[64,128]{1,0:T(8,128)S(1)} %get-tuple-element.27), channel_id=1, source_target_pairs={{0,1},{1,0},{2,3},{3,2},{4,5},{5,4},{6,7},{7,6},{8,9},{9,8},{10,11... | collective-permute-start | bytes 98312 | tf_op jit(solution)/shard_map/ppermute | solution.py:359
  12.2 2.6 %shard_map.18 = (f32[5,576,128]{2,1,0:T(8,128)S(1)}, f32[2,2,5,8,128]{4,3,2,1,0:T(8,128)S(1)}) custom-call(f32[5,576,128]{2,1,0:T(8,128)S(1)} %get-tuple-element.22.lines_ref), custom_call_target="tpu_custom_call" | custom-call | flops 1000000000 | bytes 4194304 | tf_op jit(solution)/shard_map/pallas_call | solution.py:375
  14.9 0.0 collective-permute-done.first_ref
  14.9 0.0 collective-permute-done.1.far_ref
  14.9 0.0 collective-permute-done.2.second_ref
  14.9 0.8 %shard_map.19 = (f32[5,512,128]{2,1,0:T(8,128)S(1)}, f32[60,8,128]{2,1,0:T(8,128)S(1)}, f32[61,8,128]{2,1,0:T(8,128)S(1)}) custom-call(f32[5,576,128]{2,1,0:T(8,128)S(1)} %get-tuple-element.22.lines_ref, f32[5,576,128]{2,1,0:T(8,128)S(1)} %get-tuple-element.23.new_ref, f32[2,2,5,8,128]{4,3,2,1,0:T(8,128)S(1)} %get-tuple-element.24.rim_ref, ...), custom_call_target="tpu_custom_call" | custom-call | flops 10000000 | bytes 4194304 | tf_op jit(solution)/shard_map/pallas_call | solution.py:376
  15.7 0.8 %collective-permute-start.3 = (f32[61,8,128]{2,1,0:T(8,128)S(1)}, f32[61,8,128]{2,1,0:T(8,128)S(1)}, u32[]{:S(2)}, u32[]{:S(2)}) collective-permute-start(f32[61,8,128]{2,1,0:T(8,128)S(1)} %get-tuple-element.37), channel_id=1, source_target_pairs={{0,31},{1,2},{2,1},{3,4},{4,3},{5,6},{6,5},{7,8},{8,7},{9,10},{10,... | collective-permute-start | bytes 749576 | tf_op jit(solution)/shard_map/ppermute | solution.py:364
  16.5 2.1 %shard_map.20 = (f32[5,4,10,8,128]{4,3,2,1,0:T(8,128)S(1)}, f32[8,2,5,8,128]{4,3,2,1,0:T(8,128)S(1)}) custom-call(f32[5,512,128]{2,1,0:T(8,128)S(1)} %get-tuple-element.32.rows_ref), custom_call_target="tpu_custom_call" | custom-call | flops 1000000000 | bytes 4194304 | tf_op jit(solution)/shard_map/pallas_call | solution.py:381
  18.6 0.1 collective-permute-start.4
  18.7 1.5 %collective-permute-done.4.halo_ref = f32[60,8,128]{2,1,0:T(8,128)S(1)} collective-permute-done((f32[60,8,128]{2,1,0:T(8,128)S(1)}, f32[60,8,128]{2,1,0:T(8,128)S(1)}, u32[]{:S(2)}, u32[]{:S(2)}) %collective-permute-start.4) | collective-permute-done | bytes 245792 | tf_op jit(solution)/shard_map/ppermute | solution.py:349
  20.2 1.4 %shard_map.22.part_ref = f32[5,32,2,8,128]{4,3,2,1,0:T(8,128)} custom-call(f32[5,512,128]{2,1,0:T(8,128)S(1)} %get-tuple-element.32.rows_ref, f32[5,4,10,8,128]{4,3,2,1,0:T(8,128)S(1)} %get-tuple-element.33.odd_ref, f32[8,2,5,8,128]{4,3,2,1,0:T(8,128)S(1)} %get-tuple-element.34.odd_rim_ref, f32[5,4,10,8,128]{4,3,2,1,0:T(8,128)S(1)} %get-tuple-element.35.even_ref, ...), custom_call_target="tpu_custom_call" | custom-call | flops 10000000 | bytes 1048576 | tf_op jit(solution)/shard_map/pallas_call | solution.py:387
  21.6 1.9 %collective-permute-done.3.halo_ref = f32[61,8,128]{2,1,0:T(8,128)S(1)} collective-permute-done((f32[61,8,128]{2,1,0:T(8,128)S(1)}, f32[61,8,128]{2,1,0:T(8,128)S(1)}, u32[]{:S(2)}, u32[]{:S(2)}) %collective-permute-start.3) | collective-permute-done | bytes 249888 | tf_op jit(solution)/shard_map/ppermute | solution.py:364
  23.6 1.4 %shard_map.23 = f32[5,32,2,8,128]{4,3,2,1,0:T(8,128)} custom-call(f32[5,512,128]{2,1,0:T(8,128)S(1)} %get-tuple-element.32.rows_ref, f32[5,4,10,8,128]{4,3,2,1,0:T(8,128)S(1)} %get-tuple-element.33.odd_ref, f32[8,2,5,8,128]{4,3,2,1,0:T(8,128)S(1)} %get-tuple-element.34.odd_rim_ref, ...), custom_call_target="tpu_custom_call", output_to_operand_aliasing={{}: (6, {})} | custom-call | flops 10000000 | bytes 4194304 | tf_op jit(solution)/shard_map/pallas_call | solution.py:388
  (1 shorter events, 0.0 us)
Async XLA Ops:
  1.7 13.2 %collective-permute-start = (f32[64,128]{1,0:T(8,128)S(1)}, f32[64,128]{1,0:T(8,128)S(1)}, u32[]{:S(2)}, u32[]{:S(2)}) collective-permute-start(f32[64,128]{1,0:T(8,128)S(1)} %get-tuple-element.25), channel_id=1, source_target_pairs={{0,32},{1,33},{2,34},{3,35},{4,36},{5,37},{6,38},{7,39},{8,40},{9,... | collective-permute-start | bytes 98312 | tf_op jit(solution)/shard_map/ppermute | solution.py:359
  3.1 11.8 %collective-permute-start.1 = (f32[64,128]{1,0:T(8,128)S(1)}, f32[64,128]{1,0:T(8,128)S(1)}, u32[]{:S(2)}, u32[]{:S(2)}) collective-permute-start(f32[64,128]{1,0:T(8,128)S(1)} %get-tuple-element.26), channel_id=1, source_target_pairs={{0,224},{32,64},{64,32},{96,128},{128,96},{160,192},{192,160},{224... | collective-permute-start | bytes 98312 | tf_op jit(solution)/shard_map/ppermute | solution.py:364
  11.9 3.0 %collective-permute-start.2 = (f32[64,128]{1,0:T(8,128)S(1)}, f32[64,128]{1,0:T(8,128)S(1)}, u32[]{:S(2)}, u32[]{:S(2)}) collective-permute-start(f32[64,128]{1,0:T(8,128)S(1)} %get-tuple-element.27), channel_id=1, source_target_pairs={{0,1},{1,0},{2,3},{3,2},{4,5},{5,4},{6,7},{7,6},{8,9},{9,8},{10,11... | collective-permute-start | bytes 98312 | tf_op jit(solution)/shard_map/ppermute | solution.py:359
  15.7 7.9 %collective-permute-start.3 = (f32[61,8,128]{2,1,0:T(8,128)S(1)}, f32[61,8,128]{2,1,0:T(8,128)S(1)}, u32[]{:S(2)}, u32[]{:S(2)}) collective-permute-start(f32[61,8,128]{2,1,0:T(8,128)S(1)} %get-tuple-element.37), channel_id=1, source_target_pairs={{0,31},{1,2},{2,1},{3,4},{4,3},{5,6},{6,5},{7,8},{8,7},{9,10},{10,... | collective-permute-start | bytes 749576 | tf_op jit(solution)/shard_map/ppermute | solution.py:364
  18.6 1.6 %collective-permute-start.4 = (f32[60,8,128]{2,1,0:T(8,128)S(1)}, f32[60,8,128]{2,1,0:T(8,128)S(1)}, u32[]{:S(2)}, u32[]{:S(2)}) collective-permute-start(f32[60,8,128]{2,1,0:T(8,128)S(1)} %get-tuple-element.38), channel_id=1, source_target_pairs={{0,1},{1,0},{2,3},{3,2},{4,5},{5,4},{6,7},{7,6},{8,9},{9,8},{10,11... | collective-permute-start | bytes 737288 | tf_op jit(solution)/shard_map/ppermute | solution.py:349

commit v6 on v5

--- a/solution.py
+++ b/solution.py
@@ -175,19 +175,50 @@
     return [[rim_ref[which, i, f] for f in range(5)] for i in range(2)]
 
 
-def inner_y(lines_ref, new_ref, rim_ref):
-    for at in range(0, 58, Y_CHUNK):
-        cells = [
-            jnp.stack([tile(lines_ref, f, at + k) for k in range(Y_CHUNK + 6)]) for f in range(5)
-        ]
-        new, low, high = inner(cells, Y_CHUNK, 2)
-        if at == 0:
-            keep(rim_ref, 0, low)
-        if at + Y_CHUNK == 58:
-            keep(rim_ref, 1, high)
+def starts_early():
+    return (lax.axis_index("row") == 0) & (lax.axis_index("col") < 8) & (lax.rem(lax.axis_index("col"), 2) == 1)
+
+
+def chunk(lines_ref, at):
+    cells = [
+        jnp.stack([tile(lines_ref, f, at + k) for k in range(Y_CHUNK + 6)]) for f in range(5)
+    ]
+    return inner(cells, Y_CHUNK, 2)
+
+
+def early_y(lines_ref, cells_ref, rim_ref):
+    @pl.when(starts_early())
+    def _():
+        new, low, _ = chunk(lines_ref, 0)
+        for i in range(2):
+            for f in range(5):
+                rim_ref[i, f] = low[i][f]
+        for f in range(5):
+            cells_ref[f] = new[f]
+
+
+def inner_y(lines_ref, early_ref, early_rim_ref, new_ref, rim_ref):
+    def store(new, at):
         for f in range(5):
             for k in range(Y_CHUNK):
                 new_ref[f, pl.ds(at + 3 + k, 8, stride=PITCH), :] = new[f][k]
+
+    early = starts_early()
+
+    @pl.when(early)
+    def _():
+        store([early_ref[f] for f in range(5)], 0)
+        keep(rim_ref, 0, [[early_rim_ref[i, f] for f in range(5)] for i in range(2)])
+
+    @pl.when(jnp.logical_not(early))
+    def _():
+        new, low, _ = chunk(lines_ref, 0)
+        keep(rim_ref, 0, low)
+        store(new, 0)
+
+    new, _, high = chunk(lines_ref, Y_CHUNK)
+    keep(rim_ref, 1, high)
+    store(new, Y_CHUNK)
 
 
 def outer_y(lines_ref, new_ref, rim_ref, first_ref, far_ref, second_ref, rows_ref, znear_ref, zfar_ref, ext_ref, rim_rows_ref):
@@ -233,6 +264,7 @@
     odd = lax.rem(lax.axis_index("col"), 2)
     message_z(rows_ref, znear_ref, 13 - 13 * odd)
     message_z(rows_ref, zfar_ref, 13 * odd)
+    zfar_ref[PAD - 1] = jnp.zeros((8, 128), F32)
 
 
 def message_z(rows_ref, message_ref, base):
@@ -262,8 +294,7 @@
         lax.fori_loop(0, 4, step, 0)
 
 
-def finish(side, rows_ref, new_ref, rim_ref, halo_ref, out_ref, half_ref, sems):
-    flat_ref, blocks_ref = half_ref, half_ref.reshape(5, 32, 8, 128)
+def half_z(side, rows_ref, new_ref, rim_ref, halo_ref, half_ref):
     sides = []
     for g in range(4):
         row = 128 * g
@@ -273,64 +304,69 @@
             halo = halo_ref[pl.ds((4 * f + g) * 3, 3)]
             cells.append(jnp.concatenate((halo, own) if side == 0 else (own, halo)))
         sides.append((outer_low, outer_high)[side](cells, kept(rim_ref, 2 * g + side), 3))
-    copies = []
     for g in range(4):
         for f in range(5):
             for z in range(3):
-                flat_ref[f, pl.ds(64 * g + (0, 5)[side] + z, 8, stride=8), :] = sides[g][f][z]
+                half_ref[f, pl.ds(64 * g + (0, 5)[side] + z, 8, stride=8), :] = sides[g][f][z]
             for z in range(5):
-                flat_ref[f, pl.ds(64 * g + (3, 0)[side] + z, 8, stride=8), :] = new_ref[
+                half_ref[f, pl.ds(64 * g + (3, 0)[side] + z, 8, stride=8), :] = new_ref[
                     f, g, (0, 5)[side] + z
                 ]
-        copies.append(
-            pltpu.make_async_copy(
-                blocks_ref.at[:, pl.ds(8 * g, 8)], out_ref.at[:, pl.ds(8 * g, 8), side], sems.at[g]
+        yield g
+
+
+def near_z(rows_ref, odd_ref, odd_rim_ref, even_ref, even_rim_ref, halo_ref, half_ref):
+    odd = lax.rem(lax.axis_index("col"), 2) == 1
+
+    @pl.when(odd)
+    def _():
+        list(half_z(0, rows_ref, odd_ref, odd_rim_ref, halo_ref, half_ref))
+
+    @pl.when(jnp.logical_not(odd))
+    def _():
+        list(half_z(1, rows_ref, even_ref, even_rim_ref, halo_ref, half_ref))
+
+
+def far_z(
+    rows_ref, odd_ref, odd_rim_ref, even_ref, even_rim_ref, halo_ref, near_ref, out_ref, half_ref, sems
+):
+    def work(side, new_ref, rim_ref):
+        def send(from_ref, start, size, to, sem):
+            copy = pltpu.make_async_copy(
+                from_ref.reshape(5, 32, 8, 128).at[:, pl.ds(start, size)],
+                out_ref.at[:, pl.ds(start, size), to],
+                sems.at[sem],
             )
-        )
-        copies[g].start()
-    for copy in copies:
-        copy.wait()
-
-
-def near_z(rows_ref, odd_ref, odd_rim_ref, even_ref, even_rim_ref, halo_ref, *refs):
+            copy.start()
+            return copy
+
+        copies = [send(near_ref, 0, 32, 1 - side, 4)]
+        for g in half_z(side, rows_ref, new_ref, rim_ref, halo_ref, half_ref):
+            copies.append(send(half_ref, 8 * g, 8, side, g))
+        for copy in copies:
+            copy.wait()
+
     odd = lax.rem(lax.axis_index("col"), 2) == 1
 
     @pl.when(odd)
     def _():
-        finish(0, rows_ref, odd_ref, odd_rim_ref, halo_ref, *refs)
+        work(1, odd_ref, odd_rim_ref)
 
     @pl.when(jnp.logical_not(odd))
     def _():
-        finish(1, rows_ref, even_ref, even_rim_ref, halo_ref, *refs)
-
-
-def far_z(rows_ref, odd_ref, odd_rim_ref, even_ref, even_rim_ref, halo_ref, part_ref, *refs):
-    del part_ref
-    odd = lax.rem(lax.axis_index("col"), 2) == 1
-
-    @pl.when(odd)
-    def _():
-        finish(1, rows_ref, odd_ref, odd_rim_ref, halo_ref, *refs)
-
-    @pl.when(jnp.logical_not(odd))
-    def _():
-        finish(0, rows_ref, even_ref, even_rim_ref, halo_ref, *refs)
+        work(0, even_ref, even_rim_ref)
 
 
 def array(*shape):
     return jax.ShapeDtypeStruct(shape, F32)
 
 
-def kernel(body, outs, scratch=(), sems=0, flops=10**7, outside=None, room=24, carried=None, moved=1 << 22):
+def kernel(body, outs, scratch=(), sems=0, flops=10**7, outside=None, room=24, moved=1 << 22):
     specs = {}
     if outside == "in":
         specs["in_specs"] = [pl.BlockSpec(memory_space=pltpu.HBM)]
     if outside == "out":
         specs["out_specs"] = pl.BlockSpec(memory_space=pltpu.HBM)
-    if carried is not None:
-        vmem, hbm = pl.BlockSpec(memory_space=pltpu.VMEM), pl.BlockSpec(memory_space=pltpu.HBM)
-        specs["in_specs"] = [vmem] * carried + [hbm]
-        specs["input_output_aliases"] = {carried: 0}
     scratch = [pltpu.VMEM(s, F32) for s in scratch]
     if sems:
         scratch.append(pltpu.SemaphoreType.DMA((sems,)))
@@ -369,10 +405,12 @@
     lines, near, far, again = kernel(
         pack_y, (array(*LINES), array(*HALO), array(*HALO), array(*HALO)), [ROWS], 5, outside="in"
     )(x)
+    ahead = kernel(early_y, (array(5, Y_CHUNK, 8, 128), array(2, 5, 8, 128)))(lines)
+    ahead, lines, near, far, again = lax.optimization_barrier((ahead, lines, near, far, again))
     first = near_rows(near, 0)
     far = pairs_far(far, "row")
     second = near_rows(again, 4)
-    new, rim = kernel(inner_y, (array(*LINES), array(2, 2, 5, 8, 128)), flops=10**9)(lines)
+    new, rim = kernel(inner_y, (array(*LINES), array(2, 2, 5, 8, 128)), flops=10**9)(lines, *ahead)
     rows, near, far = kernel(outer_y, (array(*ROWS), array(60, 8, 128), array(PAD, 8, 128)), [(5, 6, 8, 128), (5, 128, 128)])(
         lines, new, rim, first, far, second
     )
@@ -382,10 +420,9 @@
     odd, rows, near = lax.optimization_barrier((odd, rows, near))
     near = pairs_near(near, "col")
     even = kernel(functools.partial(inner_z, odd=0), inner_cells, flops=1000000000, moved=4194304)(rows)
-    split = array(5, 32, 2, 8, 128)
-    half = [(5, 256, 128)]
-    part = kernel(near_z, split, half, 4, outside="out", flops=10000000, moved=1048576)(rows, *odd, *even, near)
-    out = kernel(far_z, split, half, 4, outside="out", carried=6)(rows, *odd, *even, far, part)
+    half = (5, 256, 128)
+    part = kernel(near_z, array(*half))(rows, *odd, *even, near)
+    out = kernel(far_z, array(5, 32, 2, 8, 128), [half], 5, outside="out")(rows, *odd, *even, far, part)
     return out.reshape(fields.shape)
 
 

time: 25.1 us -> 24.7 us (0.984)
  the two profiles are of different devices: /device:TPU:7 before, /device:TPU:24 now
where the time goes in v6:
time: 24.7 us; the launch traced here: 24.4 us
  starting transfers between devices  12.1 us (49%)
  Pallas kernels  9.41 us (38%)
  waiting for transfers between devices  2.82 us (11%)
    ppermute x2, starting transfers between devices, pairs_far(): lax.ppermute(values, axis, [(i, (i + 1 if i % 2 else i - 1) % size) for i...  11.1 us
    ppermute x2, waiting for transfers between devices, pairs_far(): lax.ppermute(values, axis, [(i, (i + 1 if i % 2 else i - 1) % size) for i...  2.81 us
    pallas_call x1, Pallas kernels, on_device(): kernel(inner_y, (array(*LINES), array(2, 2, 5, 8, 128)), flops=10 ** 9)  2.67 us
    pallas_call x1, Pallas kernels, on_device(): kernel(functools.partial(inner_z, odd=0), inner_cells, flops=1000000000,...  2.15 us
    pallas_call x1, Pallas kernels, on_device(): kernel(pack_y, (array(*LINES), array(*HALO), array(*HALO), array(*HALO)),...  1.71 us
    pallas_call x1, Pallas kernels, on_device(): kernel(far_z, array(5, 32, 2, 8, 128), [half], 5, outside='out')  1.44 us
    ppermute x2, starting transfers between devices, near_rows(): return lax.ppermute(values, ('row', 'col'), steps)  0.98 us
    pallas_call x1, Pallas kernels, on_device(): kernel(outer_y, (array(*ROWS), array(60, 8, 128), array(PAD, 8, 128)), [(...  0.78 us
  transfers between devices with their start and end apart: 5, of which 2 were waited for; matrix products, arithmetic and copies ran while one was open for 0% of the time, Pallas kernels for 22%

profile of v6, /device:TPU:24, one launch (start us, length us, event | category | flops | bytes accessed | tf_op | source)
XLA Modules:
  0.0 24.4 jit_solution(6901770822655943157)
XLA Ops:
  0.0 1.7 %shard_map.17 = (f32[5,576,128]{2,1,0:T(8,128)S(1)}, f32[64,128]{1,0:T(8,128)S(1)}, f32[64,128]{1,0:T(8,128)S(1)}, f32[64,128]{1,0:T(8,128)S(1)}) custom-call(f32[5,512,128]{2,1,0:T(8,128)} %bitcast.2), custom_call_target="tpu_custom_call" | custom-call | flops 10000000 | bytes 4194304 | tf_op jit(solution)/shard_map/pallas_call | solution.py:405
  1.7 0.8 %collective-permute-start = (f32[64,128]{1,0:T(8,128)S(1)}, f32[64,128]{1,0:T(8,128)S(1)}, u32[]{:S(2)}, u32[]{:S(2)}) collective-permute-start(f32[64,128]{1,0:T(8,128)S(1)} %get-tuple-element.41), channel_id=1, source_target_pairs={{0,32},{1,33},{2,34},{3,35},{4,36},{5,37},{6,38},{7,39},{8,40},{9,... | collective-permute-start | bytes 98312 | tf_op jit(solution)/shard_map/ppermute | solution.py:395
  2.6 6.2 %collective-permute-start.1 = (f32[64,128]{1,0:T(8,128)S(1)}, f32[64,128]{1,0:T(8,128)S(1)}, u32[]{:S(2)}, u32[]{:S(2)}) collective-permute-start(f32[64,128]{1,0:T(8,128)S(1)} %get-tuple-element.42), channel_id=1, source_target_pairs={{0,224},{32,64},{64,32},{96,128},{128,96},{160,192},{192,160},{224... | collective-permute-start | bytes 98312 | tf_op jit(solution)/shard_map/ppermute | solution.py:400
  8.8 0.1 collective-permute-start.2
  8.9 2.7 %shard_map.19 = (f32[5,576,128]{2,1,0:T(8,128)S(1)}, f32[2,2,5,8,128]{4,3,2,1,0:T(8,128)S(1)}) custom-call(f32[5,576,128]{2,1,0:T(8,128)S(1)} %get-tuple-element.36.lines_ref, f32[5,29,8,128]{3,2,1,0:T(8,128)S(1)} %get-tuple-element.37.early_ref, f32[2,5,8,128]{3,2,1,0:T(8,128)S(1)} %get-tuple-element.38.early_rim_ref), custom_call_target="tpu_custom_call" | custom-call | flops 1000000000 | bytes 4194304 | tf_op jit(solution)/shard_map/pallas_call | solution.py:413
  11.6 0.0 collective-permute-done.first_ref
  11.6 0.9 %collective-permute-done.1.far_ref = f32[64,128]{1,0:T(8,128)S(1)} collective-permute-done((f32[64,128]{1,0:T(8,128)S(1)}, f32[64,128]{1,0:T(8,128)S(1)}, u32[]{:S(2)}, u32[]{:S(2)}) %collective-permute-start.1) | collective-permute-done | bytes 32800 | tf_op jit(solution)/shard_map/ppermute | solution.py:400
  12.5 0.0 collective-permute-done.2.second_ref
  12.5 0.8 %shard_map.20 = (f32[5,512,128]{2,1,0:T(8,128)S(1)}, f32[60,8,128]{2,1,0:T(8,128)S(1)}, f32[61,8,128]{2,1,0:T(8,128)S(1)}) custom-call(f32[5,576,128]{2,1,0:T(8,128)S(1)} %get-tuple-element.36.lines_ref, f32[5,576,128]{2,1,0:T(8,128)S(1)} %get-tuple-element.39.new_ref, f32[2,2,5,8,128]{4,3,2,1,0:T(8,128)S(1)} %get-tuple-element.40.rim_ref, ...), custom_call_target="tpu_custom_call" | custom-call | flops 10000000 | bytes 4194304 | tf_op jit(solution)/shard_map/pallas_call | solution.py:414
  13.3 4.9 %collective-permute-start.3 = (f32[61,8,128]{2,1,0:T(8,128)S(1)}, f32[61,8,128]{2,1,0:T(8,128)S(1)}, u32[]{:S(2)}, u32[]{:S(2)}) collective-permute-start(f32[61,8,128]{2,1,0:T(8,128)S(1)} %get-tuple-element.53), channel_id=1, source_target_pairs={{0,31},{1,2},{2,1},{3,4},{4,3},{5,6},{6,5},{7,8},{8,7},{9,10},{10,... | collective-permute-start | bytes 749576 | tf_op jit(solution)/shard_map/ppermute | solution.py:400
  18.2 0.0 collective-permute-start.4
  18.2 2.1 %shard_map.22 = (f32[5,4,10,8,128]{4,3,2,1,0:T(8,128)S(1)}, f32[8,2,5,8,128]{4,3,2,1,0:T(8,128)S(1)}) custom-call(f32[5,512,128]{2,1,0:T(8,128)S(1)} %get-tuple-element.48.rows_ref), custom_call_target="tpu_custom_call" | custom-call | flops 1000000000 | bytes 4194304 | tf_op jit(solution)/shard_map/pallas_call | solution.py:422
  20.4 0.0 collective-permute-done.4.halo_ref
  20.4 0.6 %shard_map.23.near_ref = f32[5,256,128]{2,1,0:T(8,128)S(1)} custom-call(f32[5,512,128]{2,1,0:T(8,128)S(1)} %get-tuple-element.48.rows_ref, f32[5,4,10,8,128]{4,3,2,1,0:T(8,128)S(1)} %get-tuple-element.49.odd_ref, f32[8,2,5,8,128]{4,3,2,1,0:T(8,128)S(1)} %get-tuple-element.50.odd_rim_ref, f32[5,4,10,8,128]{4,3,2,1,0:T(8,128)S(1)} %get-tuple-element.51.even_ref, ...), custom_call_target="tpu_custom_call" | custom-call | flops 10000000 | bytes 4194304 | tf_op jit(solution)/shard_map/pallas_call | solution.py:424
  21.1 1.9 %collective-permute-done.3.halo_ref = f32[61,8,128]{2,1,0:T(8,128)S(1)} collective-permute-done((f32[61,8,128]{2,1,0:T(8,128)S(1)}, f32[61,8,128]{2,1,0:T(8,128)S(1)}, u32[]{:S(2)}, u32[]{:S(2)}) %collective-permute-start.3) | collective-permute-done | bytes 249888 | tf_op jit(solution)/shard_map/ppermute | solution.py:400
  23.0 1.4 %shard_map.24 = f32[5,32,2,8,128]{4,3,2,1,0:T(8,128)} custom-call(f32[5,512,128]{2,1,0:T(8,128)S(1)} %get-tuple-element.48.rows_ref, f32[5,4,10,8,128]{4,3,2,1,0:T(8,128)S(1)} %get-tuple-element.49.odd_ref, f32[8,2,5,8,128]{4,3,2,1,0:T(8,128)S(1)} %get-tuple-element.50.odd_rim_ref, f32[5,4,10,8,128]{4,3,2,1,0:T(8,128)S(1)} %get-tuple-element.51.even_ref, ...), custom_call_target="tpu_custom_call" | custom-call | flops 10000000 | bytes 4194304 | tf_op jit(solution)/shard_map/pallas_call | solution.py:425
  (2 shorter events, 0.0 us)
Async XLA Ops:
  1.7 9.9 %collective-permute-start = (f32[64,128]{1,0:T(8,128)S(1)}, f32[64,128]{1,0:T(8,128)S(1)}, u32[]{:S(2)}, u32[]{:S(2)}) collective-permute-start(f32[64,128]{1,0:T(8,128)S(1)} %get-tuple-element.41), channel_id=1, source_target_pairs={{0,32},{1,33},{2,34},{3,35},{4,36},{5,37},{6,38},{7,39},{8,40},{9,... | collective-permute-start | bytes 98312 | tf_op jit(solution)/shard_map/ppermute | solution.py:395
  2.6 9.9 %collective-permute-start.1 = (f32[64,128]{1,0:T(8,128)S(1)}, f32[64,128]{1,0:T(8,128)S(1)}, u32[]{:S(2)}, u32[]{:S(2)}) collective-permute-start(f32[64,128]{1,0:T(8,128)S(1)} %get-tuple-element.42), channel_id=1, source_target_pairs={{0,224},{32,64},{64,32},{96,128},{128,96},{160,192},{192,160},{224... | collective-permute-start | bytes 98312 | tf_op jit(solution)/shard_map/ppermute | solution.py:400
  8.8 3.7 %collective-permute-start.2 = (f32[64,128]{1,0:T(8,128)S(1)}, f32[64,128]{1,0:T(8,128)S(1)}, u32[]{:S(2)}, u32[]{:S(2)}) collective-permute-start(f32[64,128]{1,0:T(8,128)S(1)} %get-tuple-element.43), channel_id=1, source_target_pairs={{0,1},{1,0},{2,3},{3,2},{4,5},{5,4},{6,7},{7,6},{8,9},{9,8},{10,11... | collective-permute-start | bytes 98312 | tf_op jit(solution)/shard_map/ppermute | solution.py:395
  13.3 9.7 %collective-permute-start.3 = (f32[61,8,128]{2,1,0:T(8,128)S(1)}, f32[61,8,128]{2,1,0:T(8,128)S(1)}, u32[]{:S(2)}, u32[]{:S(2)}) collective-permute-start(f32[61,8,128]{2,1,0:T(8,128)S(1)} %get-tuple-element.53), channel_id=1, source_target_pairs={{0,31},{1,2},{2,1},{3,4},{4,3},{5,6},{6,5},{7,8},{8,7},{9,10},{10,... | collective-permute-start | bytes 749576 | tf_op jit(solution)/shard_map/ppermute | solution.py:400
  18.2 2.2 %collective-permute-start.4 = (f32[60,8,128]{2,1,0:T(8,128)S(1)}, f32[60,8,128]{2,1,0:T(8,128)S(1)}, u32[]{:S(2)}, u32[]{:S(2)}) collective-permute-start(f32[60,8,128]{2,1,0:T(8,128)S(1)} %get-tuple-element.54), channel_id=1, source_target_pairs={{0,1},{1,0},{2,3},{3,2},{4,5},{5,4},{6,7},{7,6},{8,9},{9,8},{10,11... | collective-permute-start | bytes 737288 | tf_op jit(solution)/shard_map/ppermute | solution.py:385

commit v7 on v6

--- a/solution.py
+++ b/solution.py
@@ -176,7 +176,7 @@
 
 
 def starts_early():
-    return (lax.axis_index("row") == 0) & (lax.axis_index("col") < 8) & (lax.rem(lax.axis_index("col"), 2) == 1)
+    return (lax.axis_index("row") == 0) & (lax.rem(lax.axis_index("col"), 2) == 1)
 
 
 def chunk(lines_ref, at):
@@ -221,7 +221,7 @@
     store(new, Y_CHUNK)
 
 
-def outer_y(lines_ref, new_ref, rim_ref, first_ref, far_ref, second_ref, rows_ref, znear_ref, zfar_ref, ext_ref, rim_rows_ref):
+def outer_y(lines_ref, new_ref, rim_ref, first_ref, far_ref, second_ref, rows_ref, zfar_ref, ext_ref, rim_rows_ref):
     even = lax.rem(lax.axis_index("row"), 2) == 0
     near = jnp.where(lax.axis_index("row") < 4, first_ref[...], second_ref[...])
     far = far_ref[...]
@@ -262,7 +262,6 @@
             turned = jnp.concatenate(runs[b] + runs[4 + b])
             rows_ref[f, b * 128 : (b + 1) * 128, :] = turned.T
     odd = lax.rem(lax.axis_index("col"), 2)
-    message_z(rows_ref, znear_ref, 13 - 13 * odd)
     message_z(rows_ref, zfar_ref, 13 * odd)
     zfar_ref[PAD - 1] = jnp.zeros((8, 128), F32)
 
@@ -278,7 +277,7 @@
     return rows_ref[f, pl.ds(row + z, 8, stride=16), :]
 
 
-def inner_z(rows_ref, new_ref, rim_ref, *, odd):
+def inner_z(rows_ref, new_ref, rim_ref, *near_refs, odd):
     def step(g, carry):
         row = pl.multiple_of(128 * g, 128)
         cells = [jnp.stack([line_z(rows_ref, f, row, z) for z in range(16)]) for f in range(5)]
@@ -288,6 +287,9 @@
         for f in range(5):
             new_ref[f, g] = new[f]
         return carry
+
+    for ref in near_refs:
+        message_z(rows_ref, ref, 13 - 13 * lax.rem(lax.axis_index("col"), 2))
 
     @pl.when(lax.rem(lax.axis_index("col"), 2) == odd)
     def _():
@@ -411,12 +413,12 @@
     far = pairs_far(far, "row")
     second = near_rows(again, 4)
     new, rim = kernel(inner_y, (array(*LINES), array(2, 2, 5, 8, 128)), flops=10**9)(lines, *ahead)
-    rows, near, far = kernel(outer_y, (array(*ROWS), array(60, 8, 128), array(PAD, 8, 128)), [(5, 6, 8, 128), (5, 128, 128)])(
+    rows, far = kernel(outer_y, (array(*ROWS), array(PAD, 8, 128)), [(5, 6, 8, 128), (5, 128, 128)])(
         lines, new, rim, first, far, second
     )
     far = pairs_far(far, "col")
     inner_cells = (array(5, 4, 10, 8, 128), array(8, 2, 5, 8, 128))
-    odd = kernel(functools.partial(inner_z, odd=1), inner_cells, flops=1000000000, moved=4194304)(rows)
+    *odd, near = kernel(functools.partial(inner_z, odd=1), inner_cells + (array(60, 8, 128),), flops=1000000000, moved=4194304)(rows)
     odd, rows, near = lax.optimization_barrier((odd, rows, near))
     near = pairs_near(near, "col")
     even = kernel(functools.partial(inner_z, odd=0), inner_cells, flops=1000000000, moved=4194304)(rows)

time: 24.7 us -> 24.6 us (level)
  transfers between devices with their start and end apart: 5 -> 5, of which waited for: 2 -> 2; matrix products, arithmetic and copies ran while one was open for 0% -> 0% of each run, Pallas kernels for 22% -> 23%
where the time goes in v7:
time: 24.6 us; the launch traced here: 24.3 us
  starting transfers between devices  12.2 us (50%)
  Pallas kernels  9.46 us (38%)
  waiting for transfers between devices  2.59 us (11%)
    ppermute x2, starting transfers between devices, pairs_far(): lax.ppermute(values, axis, [(i, (i + 1 if i % 2 else i - 1) % size) for i...  11.1 us
    pallas_call x1, Pallas kernels, on_device(): kernel(inner_y, (array(*LINES), array(2, 2, 5, 8, 128)), flops=10 ** 9)  2.67 us
    ppermute x2, waiting for transfers between devices, pairs_far(): lax.ppermute(values, axis, [(i, (i + 1 if i % 2 else i - 1) % size) for i...  2.58 us
    pallas_call x1, Pallas kernels, on_device(): kernel(functools.partial(inner_z, odd=0), inner_cells, flops=1000000000,...  2.16 us
    pallas_call x1, Pallas kernels, on_device(): kernel(pack_y, (array(*LINES), array(*HALO), array(*HALO), array(*HALO)),...  1.71 us
    pallas_call x1, Pallas kernels, on_device(): kernel(far_z, array(5, 32, 2, 8, 128), [half], 5, outside='out')  1.44 us
    ppermute x2, starting transfers between devices, near_rows(): return lax.ppermute(values, ('row', 'col'), steps)  0.98 us
    pallas_call x1, Pallas kernels, on_device(): kernel(outer_y, (array(*ROWS), array(PAD, 8, 128)), [(5, 6, 8, 128), (5,...  0.69 us
  transfers between devices with their start and end apart: 5, of which 2 were waited for; matrix products, arithmetic and copies ran while one was open for 0% of the time, Pallas kernels for 23%

profile of v7, /device:TPU:24, one launch (start us, length us, event | category | flops | bytes accessed | tf_op | source)
XLA Modules:
  0.0 24.3 jit_solution(12552495820020373784)
XLA Ops:
  0.0 1.7 %shard_map.17 = (f32[5,576,128]{2,1,0:T(8,128)S(1)}, f32[64,128]{1,0:T(8,128)S(1)}, f32[64,128]{1,0:T(8,128)S(1)}, f32[64,128]{1,0:T(8,128)S(1)}) custom-call(f32[5,512,128]{2,1,0:T(8,128)} %bitcast.2), custom_call_target="tpu_custom_call" | custom-call | flops 10000000 | bytes 4194304 | tf_op jit(solution)/shard_map/pallas_call | solution.py:407
  1.7 0.8 %collective-permute-start = (f32[64,128]{1,0:T(8,128)S(1)}, f32[64,128]{1,0:T(8,128)S(1)}, u32[]{:S(2)}, u32[]{:S(2)}) collective-permute-start(f32[64,128]{1,0:T(8,128)S(1)} %get-tuple-element.41), channel_id=1, source_target_pairs={{0,32},{1,33},{2,34},{3,35},{4,36},{5,37},{6,38},{7,39},{8,40},{9,... | collective-permute-start | bytes 98312 | tf_op jit(solution)/shard_map/ppermute | solution.py:397
  2.6 6.2 %collective-permute-start.1 = (f32[64,128]{1,0:T(8,128)S(1)}, f32[64,128]{1,0:T(8,128)S(1)}, u32[]{:S(2)}, u32[]{:S(2)}) collective-permute-start(f32[64,128]{1,0:T(8,128)S(1)} %get-tuple-element.42), channel_id=1, source_target_pairs={{0,224},{32,64},{64,32},{96,128},{128,96},{160,192},{192,160},{224... | collective-permute-start | bytes 98312 | tf_op jit(solution)/shard_map/ppermute | solution.py:402
  8.8 0.1 collective-permute-start.2
  8.9 2.7 %shard_map.19 = (f32[5,576,128]{2,1,0:T(8,128)S(1)}, f32[2,2,5,8,128]{4,3,2,1,0:T(8,128)S(1)}) custom-call(f32[5,576,128]{2,1,0:T(8,128)S(1)} %get-tuple-element.36.lines_ref, f32[5,29,8,128]{3,2,1,0:T(8,128)S(1)} %get-tuple-element.37.early_ref, f32[2,5,8,128]{3,2,1,0:T(8,128)S(1)} %get-tuple-element.38.early_rim_ref), custom_call_target="tpu_custom_call" | custom-call | flops 1000000000 | bytes 4194304 | tf_op jit(solution)/shard_map/pallas_call | solution.py:415
  11.6 0.0 collective-permute-done.first_ref
  11.6 0.9 %collective-permute-done.1.far_ref = f32[64,128]{1,0:T(8,128)S(1)} collective-permute-done((f32[64,128]{1,0:T(8,128)S(1)}, f32[64,128]{1,0:T(8,128)S(1)}, u32[]{:S(2)}, u32[]{:S(2)}) %collective-permute-start.1) | collective-permute-done | bytes 32800 | tf_op jit(solution)/shard_map/ppermute | solution.py:402
  12.5 0.0 collective-permute-done.2.second_ref
  12.5 0.7 %shard_map.20 = (f32[5,512,128]{2,1,0:T(8,128)S(1)}, f32[61,8,128]{2,1,0:T(8,128)S(1)}) custom-call(f32[5,576,128]{2,1,0:T(8,128)S(1)} %get-tuple-element.36.lines_ref, f32[5,576,128]{2,1,0:T(8,128)S(1)} %get-tuple-element.39.new_ref, f32[2,2,5,8,128]{4,3,2,1,0:T(8,128)S(1)} %get-tuple-element.40.rim_ref, f32[64,128]{1,0:T(8,128)S(1)} %collective-permute-done.first_ref, ...), custom_call_target="tpu_custom_call" | custom-call | flops 10000000 | bytes 4194304 | tf_op jit(solution)/shard_map/pallas_call | solution.py:416
  13.2 4.9 %collective-permute-start.3 = (f32[61,8,128]{2,1,0:T(8,128)S(1)}, f32[61,8,128]{2,1,0:T(8,128)S(1)}, u32[]{:S(2)}, u32[]{:S(2)}) collective-permute-start(f32[61,8,128]{2,1,0:T(8,128)S(1)} %get-tuple-element.53), channel_id=1, source_target_pairs={{0,31},{1,2},{2,1},{3,4},{4,3},{5,6},{6,5},{7,8},{8,7},{9,10},{10,... | collective-permute-start | bytes 749576 | tf_op jit(solution)/shard_map/ppermute | solution.py:402
  18.1 0.1 shard_map.21
  18.3 0.1 collective-permute-start.4
  18.4 2.2 %shard_map.22 = (f32[5,4,10,8,128]{4,3,2,1,0:T(8,128)S(1)}, f32[8,2,5,8,128]{4,3,2,1,0:T(8,128)S(1)}) custom-call(f32[5,512,128]{2,1,0:T(8,128)S(1)} %get-tuple-element.48.rows_ref), custom_call_target="tpu_custom_call" | custom-call | flops 1000000000 | bytes 4194304 | tf_op jit(solution)/shard_map/pallas_call | solution.py:424
  20.5 0.0 collective-permute-done.4.halo_ref
  20.5 0.6 %shard_map.23.near_ref = f32[5,256,128]{2,1,0:T(8,128)S(1)} custom-call(f32[5,512,128]{2,1,0:T(8,128)S(1)} %get-tuple-element.48.rows_ref, f32[5,4,10,8,128]{4,3,2,1,0:T(8,128)S(1)} %get-tuple-element.49.odd_ref, f32[8,2,5,8,128]{4,3,2,1,0:T(8,128)S(1)} %get-tuple-element.50.odd_rim_ref, f32[5,4,10,8,128]{4,3,2,1,0:T(8,128)S(1)} %get-tuple-element.51.even_ref, ...), custom_call_target="tpu_custom_call" | custom-call | flops 10000000 | bytes 4194304 | tf_op jit(solution)/shard_map/pallas_call | solution.py:426
  21.2 1.7 %collective-permute-done.3.halo_ref = f32[61,8,128]{2,1,0:T(8,128)S(1)} collective-permute-done((f32[61,8,128]{2,1,0:T(8,128)S(1)}, f32[61,8,128]{2,1,0:T(8,128)S(1)}, u32[]{:S(2)}, u32[]{:S(2)}) %collective-permute-start.3) | collective-permute-done | bytes 249888 | tf_op jit(solution)/shard_map/ppermute | solution.py:402
  22.9 1.4 %shard_map.24 = f32[5,32,2,8,128]{4,3,2,1,0:T(8,128)} custom-call(f32[5,512,128]{2,1,0:T(8,128)S(1)} %get-tuple-element.48.rows_ref, f32[5,4,10,8,128]{4,3,2,1,0:T(8,128)S(1)} %get-tuple-element.49.odd_ref, f32[8,2,5,8,128]{4,3,2,1,0:T(8,128)S(1)} %get-tuple-element.50.odd_rim_ref, f32[5,4,10,8,128]{4,3,2,1,0:T(8,128)S(1)} %get-tuple-element.51.even_ref, ...), custom_call_target="tpu_custom_call" | custom-call | flops 10000000 | bytes 4194304 | tf_op jit(solution)/shard_map/pallas_call | solution.py:427
  (1 shorter events, 0.0 us)
Async XLA Ops:
  1.7 9.9 %collective-permute-start = (f32[64,128]{1,0:T(8,128)S(1)}, f32[64,128]{1,0:T(8,128)S(1)}, u32[]{:S(2)}, u32[]{:S(2)}) collective-permute-start(f32[64,128]{1,0:T(8,128)S(1)} %get-tuple-element.41), channel_id=1, source_target_pairs={{0,32},{1,33},{2,34},{3,35},{4,36},{5,37},{6,38},{7,39},{8,40},{9,... | collective-permute-start | bytes 98312 | tf_op jit(solution)/shard_map/ppermute | solution.py:397
  2.6 9.9 %collective-permute-start.1 = (f32[64,128]{1,0:T(8,128)S(1)}, f32[64,128]{1,0:T(8,128)S(1)}, u32[]{:S(2)}, u32[]{:S(2)}) collective-permute-start(f32[64,128]{1,0:T(8,128)S(1)} %get-tuple-element.42), channel_id=1, source_target_pairs={{0,224},{32,64},{64,32},{96,128},{128,96},{160,192},{192,160},{224... | collective-permute-start | bytes 98312 | tf_op jit(solution)/shard_map/ppermute | solution.py:402
  8.8 3.7 %collective-permute-start.2 = (f32[64,128]{1,0:T(8,128)S(1)}, f32[64,128]{1,0:T(8,128)S(1)}, u32[]{:S(2)}, u32[]{:S(2)}) collective-permute-start(f32[64,128]{1,0:T(8,128)S(1)} %get-tuple-element.43), channel_id=1, source_target_pairs={{0,1},{1,0},{2,3},{3,2},{4,5},{5,4},{6,7},{7,6},{8,9},{9,8},{10,11... | collective-permute-start | bytes 98312 | tf_op jit(solution)/shard_map/ppermute | solution.py:397
  13.2 9.7 %collective-permute-start.3 = (f32[61,8,128]{2,1,0:T(8,128)S(1)}, f32[61,8,128]{2,1,0:T(8,128)S(1)}, u32[]{:S(2)}, u32[]{:S(2)}) collective-permute-start(f32[61,8,128]{2,1,0:T(8,128)S(1)} %get-tuple-element.53), channel_id=1, source_target_pairs={{0,31},{1,2},{2,1},{3,4},{4,3},{5,6},{6,5},{7,8},{8,7},{9,10},{10,... | collective-permute-start | bytes 749576 | tf_op jit(solution)/shard_map/ppermute | solution.py:402
  18.3 2.3 %collective-permute-start.4 = (f32[60,8,128]{2,1,0:T(8,128)S(1)}, f32[60,8,128]{2,1,0:T(8,128)S(1)}, u32[]{:S(2)}, u32[]{:S(2)}) collective-permute-start(f32[60,8,128]{2,1,0:T(8,128)S(1)} %get-tuple-element.54), channel_id=1, source_target_pairs={{0,1},{1,0},{2,3},{3,2},{4,5},{5,4},{6,7},{7,6},{8,9},{9,8},{10,11... | collective-permute-start | bytes 737288 | tf_op jit(solution)/shard_map/ppermute | solution.py:387

commit v8 on v7

--- a/solution.py
+++ b/solution.py
@@ -175,50 +175,63 @@
     return [[rim_ref[which, i, f] for f in range(5)] for i in range(2)]
 
 
-def starts_early():
-    return (lax.axis_index("row") == 0) & (lax.rem(lax.axis_index("col"), 2) == 1)
-
-
-def chunk(lines_ref, at):
-    cells = [
-        jnp.stack([tile(lines_ref, f, at + k) for k in range(Y_CHUNK + 6)]) for f in range(5)
-    ]
-    return inner(cells, Y_CHUNK, 2)
+EARLY_EVEN = 7
+
+
+def early_counts():
+    row, col = lax.axis_index("row"), lax.axis_index("col")
+    odd = lax.rem(col, 2) == 1
+    return ((row == 0) & odd, Y_CHUNK), ((row == 0) & (col < 8) & jnp.logical_not(odd), EARLY_EVEN)
+
+
+def chunk(lines_ref, at, count):
+    cells = [jnp.stack([tile(lines_ref, f, at + k) for k in range(count + 6)]) for f in range(5)]
+    return inner(cells, count, 2)
 
 
 def early_y(lines_ref, cells_ref, rim_ref):
-    @pl.when(starts_early())
-    def _():
-        new, low, _ = chunk(lines_ref, 0)
-        for i in range(2):
+    for chosen, count in early_counts():
+
+        @pl.when(chosen)
+        def _():
+            new, low, _ = chunk(lines_ref, 0, count)
+            for i in range(2):
+                for f in range(5):
+                    rim_ref[i, f] = low[i][f]
             for f in range(5):
-                rim_ref[i, f] = low[i][f]
+                cells_ref[f, 0:count] = new[f]
+
+
+def inner_y(lines_ref, early_ref, early_rim_ref, new_ref, rim_ref):
+    def store(new, at, count):
         for f in range(5):
-            cells_ref[f] = new[f]
-
-
-def inner_y(lines_ref, early_ref, early_rim_ref, new_ref, rim_ref):
-    def store(new, at):
-        for f in range(5):
-            for k in range(Y_CHUNK):
+            for k in range(count):
                 new_ref[f, pl.ds(at + 3 + k, 8, stride=PITCH), :] = new[f][k]
 
-    early = starts_early()
-
-    @pl.when(early)
-    def _():
-        store([early_ref[f] for f in range(5)], 0)
-        keep(rim_ref, 0, [[early_rim_ref[i, f] for f in range(5)] for i in range(2)])
-
-    @pl.when(jnp.logical_not(early))
-    def _():
-        new, low, _ = chunk(lines_ref, 0)
-        keep(rim_ref, 0, low)
-        store(new, 0)
-
-    new, _, high = chunk(lines_ref, Y_CHUNK)
-    keep(rim_ref, 1, high)
-    store(new, Y_CHUNK)
+    def rest(at):
+        while at < 58:
+            count = min(Y_CHUNK, 58 - at)
+            new, low, high = chunk(lines_ref, at, count)
+            if at == 0:
+                keep(rim_ref, 0, low)
+            if at + count == 58:
+                keep(rim_ref, 1, high)
+            store(new, at, count)
+            at += count
+
+    neither = True
+    for chosen, count in early_counts():
+        neither = jnp.logical_and(neither, jnp.logical_not(chosen))
+
+        @pl.when(chosen)
+        def _():
+            store([early_ref[f, 0:count] for f in range(5)], 0, count)
+            keep(rim_ref, 0, [[early_rim_ref[i, f] for f in range(5)] for i in range(2)])
+            rest(count)
+
+    @pl.when(neither)
+    def _():
+        rest(0)
 
 
 def outer_y(lines_ref, new_ref, rim_ref, first_ref, far_ref, second_ref, rows_ref, zfar_ref, ext_ref, rim_rows_ref):

time: 24.6 us -> 24.7 us (level)
  no operation moved by 1% of the time
where the time goes in v8:
time: 24.7 us
  starting transfers between devices  12.4 us (50%)
  Pallas kernels  9.46 us (38%)
  waiting for transfers between devices  2.6 us (11%)
    ppermute x2, starting transfers between devices, pairs_far(): lax.ppermute(values, axis, [(i, (i + 1 if i % 2 else i - 1) % size) for i...  11.3 us
    pallas_call x1, Pallas kernels, on_device(): kernel(inner_y, (array(*LINES), array(2, 2, 5, 8, 128)), flops=10 ** 9)  2.65 us
    ppermute x2, waiting for transfers between devices, pairs_far(): lax.ppermute(values, axis, [(i, (i + 1 if i % 2 else i - 1) % size) for i...  2.59 us
    pallas_call x1, Pallas kernels, on_device(): kernel(functools.partial(inner_z, odd=0), inner_cells, flops=1000000000,...  2.16 us
    pallas_call x1, Pallas kernels, on_device(): kernel(pack_y, (array(*LINES), array(*HALO), array(*HALO), array(*HALO)),...  1.71 us
    pallas_call x1, Pallas kernels, on_device(): kernel(far_z, array(5, 32, 2, 8, 128), [half], 5, outside='out')  1.44 us
    ppermute x2, starting transfers between devices, near_rows(): return lax.ppermute(values, ('row', 'col'), steps)  0.98 us
    pallas_call x1, Pallas kernels, on_device(): kernel(outer_y, (array(*ROWS), array(PAD, 8, 128)), [(5, 6, 8, 128), (5,...  0.69 us
  transfers between devices with their start and end apart: 5, of which 2 were waited for; matrix products, arithmetic and copies ran while one was open for 0% of the time, Pallas kernels for 23%

profile of v8, /device:TPU:24, one launch (start us, length us, event | category | flops | bytes accessed | tf_op | source)
XLA Modules:
  0.0 24.7 jit_solution(4484429147057693405)
XLA Ops:
  0.0 1.7 %shard_map.17 = (f32[5,576,128]{2,1,0:T(8,128)S(1)}, f32[64,128]{1,0:T(8,128)S(1)}, f32[64,128]{1,0:T(8,128)S(1)}, f32[64,128]{1,0:T(8,128)S(1)}) custom-call(f32[5,512,128]{2,1,0:T(8,128)} %bitcast.2), custom_call_target="tpu_custom_call" | custom-call | flops 10000000 | bytes 4194304 | tf_op jit(solution)/shard_map/pallas_call | solution.py:420
  1.7 0.8 %collective-permute-start = (f32[64,128]{1,0:T(8,128)S(1)}, f32[64,128]{1,0:T(8,128)S(1)}, u32[]{:S(2)}, u32[]{:S(2)}) collective-permute-start(f32[64,128]{1,0:T(8,128)S(1)} %get-tuple-element.41), channel_id=1, source_target_pairs={{0,32},{1,33},{2,34},{3,35},{4,36},{5,37},{6,38},{7,39},{8,40},{9,... | collective-permute-start | bytes 98312 | tf_op jit(solution)/shard_map/ppermute | solution.py:410
  2.6 6.2 %collective-permute-start.1 = (f32[64,128]{1,0:T(8,128)S(1)}, f32[64,128]{1,0:T(8,128)S(1)}, u32[]{:S(2)}, u32[]{:S(2)}) collective-permute-start(f32[64,128]{1,0:T(8,128)S(1)} %get-tuple-element.42), channel_id=1, source_target_pairs={{0,224},{32,64},{64,32},{96,128},{128,96},{160,192},{192,160},{224... | collective-permute-start | bytes 98312 | tf_op jit(solution)/shard_map/ppermute | solution.py:415
  8.8 0.1 collective-permute-start.2
  8.9 2.7 %shard_map.19 = (f32[5,576,128]{2,1,0:T(8,128)S(1)}, f32[2,2,5,8,128]{4,3,2,1,0:T(8,128)S(1)}) custom-call(f32[5,576,128]{2,1,0:T(8,128)S(1)} %get-tuple-element.36.lines_ref, f32[5,29,8,128]{3,2,1,0:T(8,128)S(1)} %get-tuple-element.37.early_ref, f32[2,5,8,128]{3,2,1,0:T(8,128)S(1)} %get-tuple-element.38.early_rim_ref), custom_call_target="tpu_custom_call" | custom-call | flops 1000000000 | bytes 4194304 | tf_op jit(solution)/shard_map/pallas_call | solution.py:428
  11.6 0.0 collective-permute-done.first_ref
  11.6 0.9 %collective-permute-done.1.far_ref = f32[64,128]{1,0:T(8,128)S(1)} collective-permute-done((f32[64,128]{1,0:T(8,128)S(1)}, f32[64,128]{1,0:T(8,128)S(1)}, u32[]{:S(2)}, u32[]{:S(2)}) %collective-permute-start.1) | collective-permute-done | bytes 32800 | tf_op jit(solution)/shard_map/ppermute | solution.py:415
  12.5 0.0 collective-permute-done.2.second_ref
  12.5 0.7 %shard_map.20 = (f32[5,512,128]{2,1,0:T(8,128)S(1)}, f32[61,8,128]{2,1,0:T(8,128)S(1)}) custom-call(f32[5,576,128]{2,1,0:T(8,128)S(1)} %get-tuple-element.36.lines_ref, f32[5,576,128]{2,1,0:T(8,128)S(1)} %get-tuple-element.39.new_ref, f32[2,2,5,8,128]{4,3,2,1,0:T(8,128)S(1)} %get-tuple-element.40.rim_ref, f32[64,128]{1,0:T(8,128)S(1)} %collective-permute-done.first_ref, ...), custom_call_target="tpu_custom_call" | custom-call | flops 10000000 | bytes 4194304 | tf_op jit(solution)/shard_map/pallas_call | solution.py:429
  13.2 5.1 %collective-permute-start.3 = (f32[61,8,128]{2,1,0:T(8,128)S(1)}, f32[61,8,128]{2,1,0:T(8,128)S(1)}, u32[]{:S(2)}, u32[]{:S(2)}) collective-permute-start(f32[61,8,128]{2,1,0:T(8,128)S(1)} %get-tuple-element.53), channel_id=1, source_target_pairs={{0,31},{1,2},{2,1},{3,4},{4,3},{5,6},{6,5},{7,8},{8,7},{9,10},{10,... | collective-permute-start | bytes 749576 | tf_op jit(solution)/shard_map/ppermute | solution.py:415
  18.3 0.1 shard_map.21
  18.4 0.1 collective-permute-start.4
  18.5 2.2 %shard_map.22 = (f32[5,4,10,8,128]{4,3,2,1,0:T(8,128)S(1)}, f32[8,2,5,8,128]{4,3,2,1,0:T(8,128)S(1)}) custom-call(f32[5,512,128]{2,1,0:T(8,128)S(1)} %get-tuple-element.48.rows_ref), custom_call_target="tpu_custom_call" | custom-call | flops 1000000000 | bytes 4194304 | tf_op jit(solution)/shard_map/pallas_call | solution.py:437
  20.7 0.0 collective-permute-done.4.halo_ref
  20.7 0.6 %shard_map.23.near_ref = f32[5,256,128]{2,1,0:T(8,128)S(1)} custom-call(f32[5,512,128]{2,1,0:T(8,128)S(1)} %get-tuple-element.48.rows_ref, f32[5,4,10,8,128]{4,3,2,1,0:T(8,128)S(1)} %get-tuple-element.49.odd_ref, f32[8,2,5,8,128]{4,3,2,1,0:T(8,128)S(1)} %get-tuple-element.50.odd_rim_ref, f32[5,4,10,8,128]{4,3,2,1,0:T(8,128)S(1)} %get-tuple-element.51.even_ref, ...), custom_call_target="tpu_custom_call" | custom-call | flops 10000000 | bytes 4194304 | tf_op jit(solution)/shard_map/pallas_call | solution.py:439
  21.4 1.7 %collective-permute-done.3.halo_ref = f32[61,8,128]{2,1,0:T(8,128)S(1)} collective-permute-done((f32[61,8,128]{2,1,0:T(8,128)S(1)}, f32[61,8,128]{2,1,0:T(8,128)S(1)}, u32[]{:S(2)}, u32[]{:S(2)}) %collective-permute-start.3) | collective-permute-done | bytes 249888 | tf_op jit(solution)/shard_map/ppermute | solution.py:415
  23.1 1.4 %shard_map.24 = f32[5,32,2,8,128]{4,3,2,1,0:T(8,128)} custom-call(f32[5,512,128]{2,1,0:T(8,128)S(1)} %get-tuple-element.48.rows_ref, f32[5,4,10,8,128]{4,3,2,1,0:T(8,128)S(1)} %get-tuple-element.49.odd_ref, f32[8,2,5,8,128]{4,3,2,1,0:T(8,128)S(1)} %get-tuple-element.50.odd_rim_ref, f32[5,4,10,8,128]{4,3,2,1,0:T(8,128)S(1)} %get-tuple-element.51.even_ref, ...), custom_call_target="tpu_custom_call" | custom-call | flops 10000000 | bytes 4194304 | tf_op jit(solution)/shard_map/pallas_call | solution.py:440
  (1 shorter events, 0.0 us)
Async XLA Ops:
  1.7 9.9 %collective-permute-start = (f32[64,128]{1,0:T(8,128)S(1)}, f32[64,128]{1,0:T(8,128)S(1)}, u32[]{:S(2)}, u32[]{:S(2)}) collective-permute-start(f32[64,128]{1,0:T(8,128)S(1)} %get-tuple-element.41), channel_id=1, source_target_pairs={{0,32},{1,33},{2,34},{3,35},{4,36},{5,37},{6,38},{7,39},{8,40},{9,... | collective-permute-start | bytes 98312 | tf_op jit(solution)/shard_map/ppermute | solution.py:410
  2.6 9.9 %collective-permute-start.1 = (f32[64,128]{1,0:T(8,128)S(1)}, f32[64,128]{1,0:T(8,128)S(1)}, u32[]{:S(2)}, u32[]{:S(2)}) collective-permute-start(f32[64,128]{1,0:T(8,128)S(1)} %get-tuple-element.42), channel_id=1, source_target_pairs={{0,224},{32,64},{64,32},{96,128},{128,96},{160,192},{192,160},{224... | collective-permute-start | bytes 98312 | tf_op jit(solution)/shard_map/ppermute | solution.py:415
  8.8 3.7 %collective-permute-start.2 = (f32[64,128]{1,0:T(8,128)S(1)}, f32[64,128]{1,0:T(8,128)S(1)}, u32[]{:S(2)}, u32[]{:S(2)}) collective-permute-start(f32[64,128]{1,0:T(8,128)S(1)} %get-tuple-element.43), channel_id=1, source_target_pairs={{0,1},{1,0},{2,3},{3,2},{4,5},{5,4},{6,7},{7,6},{8,9},{9,8},{10,11... | collective-permute-start | bytes 98312 | tf_op jit(solution)/shard_map/ppermute | solution.py:410
  13.2 9.8 %collective-permute-start.3 = (f32[61,8,128]{2,1,0:T(8,128)S(1)}, f32[61,8,128]{2,1,0:T(8,128)S(1)}, u32[]{:S(2)}, u32[]{:S(2)}) collective-permute-start(f32[61,8,128]{2,1,0:T(8,128)S(1)} %get-tuple-element.53), channel_id=1, source_target_pairs={{0,31},{1,2},{2,1},{3,4},{4,3},{5,6},{6,5},{7,8},{8,7},{9,10},{10,... | collective-permute-start | bytes 749576 | tf_op jit(solution)/shard_map/ppermute | solution.py:415
  18.4 2.3 %collective-permute-start.4 = (f32[60,8,128]{2,1,0:T(8,128)S(1)}, f32[60,8,128]{2,1,0:T(8,128)S(1)}, u32[]{:S(2)}, u32[]{:S(2)}) collective-permute-start(f32[60,8,128]{2,1,0:T(8,128)S(1)} %get-tuple-element.54), channel_id=1, source_target_pairs={{0,1},{1,0},{2,3},{3,2},{4,5},{5,4},{6,7},{7,6},{8,9},{9,8},{10,11... | collective-permute-start | bytes 737288 | tf_op jit(solution)/shard_map/ppermute | solution.py:400
